TPU v7x, 128 devices: a whole 4x4x4 slice. The times are simulated.
128 devices in a mesh: replica: 32 (over x, y, core), fsdp: 4 (over z).
Axes of the slice: x: 4, y: 4, z: 4, core: 2. Of those that a mesh axis runs over, the one named last changes fastest.
Arguments:
- local_weights: bfloat16 [32, 2, 512, 8192], P('replica', None, 'fsdp'), may hold values from -100000 to 100000
- global_weights: float32 [2, 512, 8192], P(None, 'fsdp'), may hold values from -6 to 6
- momentum: float32 [2, 512, 8192], P(None, 'fsdp', 'replica'), may hold values from -6 to 6
Outputs:
- refreshed: float32 [2, 512, 8192], P(None, 'fsdp')
- new_momentum: float32 [2, 512, 8192], P(None, 'fsdp', 'replica')
All inputs are finite; a program needn't handle non-finite values. Where the computation divides by a largest or mean magnitude, that divisor is 1e-20 or more.
Results may differ from a plain program's by a relative error of at most 0.012.
Values may be sent and summed in bfloat16 or wider, within the bound.
A program may use at most 128 MiB of HBM per device.

v0:
```python
import jax
import jax.numpy as jnp
from jax import lax
from jax.sharding import PartitionSpec as P

OUTER_MOMENTUM = 0.9
OUTER_RATE = 0.7
CLIP_LEVEL = 1.0
SCALE_EPSILON = 1e-06


def quantize(values):
    blocks = values.reshape(values.shape[:-1] + (values.shape[-1] // 64, 64))
    scales = (jnp.max(jnp.abs(blocks), axis=-1) + SCALE_EPSILON).astype(jnp.bfloat16)
    encoded = (blocks / scales.astype(jnp.float32)[..., None]).astype(jnp.bfloat16)
    return (encoded.reshape(values.shape), scales)


def restore(encoded, scales):
    blocks = encoded.astype(jnp.float32).reshape(encoded.shape[:-1] + (encoded.shape[-1] // 64, 64))
    return (blocks * scales.astype(jnp.float32)[..., None]).reshape(encoded.shape)


def synchronize(local_weights, global_weights, momentum):
    replicas = lax.axis_size("replica")
    difference = global_weights - local_weights[0].astype(jnp.float32)
    block_codes, block_scales = quantize(difference)
    arrived_codes, arrived_scales = (
        lax.all_to_all(block_codes[None], "replica", split_axis=3, concat_axis=0, tiled=True),
        lax.all_to_all(block_scales[None], "replica", split_axis=3, concat_axis=0, tiled=True),
    )
    owner_total = jnp.sum(restore(arrived_codes, arrived_scales), axis=0)
    average = owner_total / replicas
    squares = jnp.sum(average * average, axis=(1, 2))
    norm_squared = lax.psum(squares, ("replica", "fsdp"))
    element_count = global_weights.shape[1] * lax.axis_size("fsdp") * global_weights.shape[2]
    factor = jnp.minimum(
        1.0, CLIP_LEVEL * jnp.sqrt(jnp.float32(element_count)) / jnp.sqrt(norm_squared + 1e-06)
    )
    clipped = average * factor[:, None, None]
    moment = OUTER_MOMENTUM * momentum + clipped
    outer_step = clipped + OUTER_MOMENTUM * moment
    step_codes, step_scales = quantize(outer_step)
    all_codes, all_scales = (
        lax.all_gather(step_codes, "replica", axis=2, tiled=True),
        lax.all_gather(step_scales, "replica", axis=2, tiled=True),
    )
    refreshed = global_weights - OUTER_RATE * restore(all_codes, all_scales)
    return (refreshed, moment)


def local(local_weights, global_weights, momentum):
    synced = [
        synchronize(
            local_weights[:, fragment : fragment + 1],
            global_weights[fragment : fragment + 1],
            momentum[fragment : fragment + 1],
        )
        for fragment in range(global_weights.shape[0])
    ]
    refreshed = jnp.concatenate([entry[0] for entry in synced], axis=0)
    moment = jnp.concatenate([entry[1] for entry in synced], axis=0)
    return (refreshed, moment)


def solution(mesh):
    return jax.shard_map(
        local,
        mesh=mesh,
        in_specs=(
            P("replica", None, "fsdp", None),
            P(None, "fsdp", None),
            P(None, "fsdp", "replica"),
        ),
        out_specs=(P(None, "fsdp", None), P(None, "fsdp", "replica")),
        check_vma=False,
    )
```

profile of v0, /device:TPU:1, one launch (start us, length us, event | category | flops | bytes accessed | tf_op | source)
XLA Modules:
  0.0 477.6 jit_solution(4572888085766426700)
XLA Ops:
  7.2 7.7 %fusion.20 = (f32[1,128,8192]{2,1,0:T(8,128)}, f32[1,128,8192]{2,1,0:T(8,128)}) fusion(f32[2,128,8192]{2,1,0:T(8,128)} %param.4), kind=kLoop, calls=%fused_computation.46 | loop fusion | bytes 16777216 | tf_op jit(solution)/shard_map/slice | solution.py:56
  14.9 5.6 %copy.60 = f32[1,128,8192]{1,2,0:T(8,128)} copy(f32[1,128,8192]{2,1,0:T(8,128)} %get-tuple-element.12) | data formatting | bytes 8388608
  20.5 4.6 fusion.21
  25.1 3.2 copy.61
  28.3 4.6 fusion.6
  32.9 2.9 reduce_max.36
  37.9 8.6 %all-to-all-start.1 = ((bf16[32,2,256]{2,1,0:T(2,128)(2,1)}), bf16[32,2,256]{2,1,0:T(2,128)(2,1)S(1)}, u32[]{:S(2)}, u32[]{:S(2)}) async-start(bf16[32,2,256]{2,1,0:T(2,128)(2,1)} %reshape.460), calls=%async_computation.1 | async-start | bytes 65536 | tf_op jit(solution)/shard_map/all_to_all | solution.py:30
  46.5 5.6 %copy.63 = f32[1,128,8192]{1,2,0:T(8,128)} copy(f32[1,128,8192]{2,1,0:T(8,128)} %get-tuple-element.13) | data formatting | bytes 8388608
  52.1 4.1 copy.64
  56.2 5.2 %fusion.7 = f32[1,128,8192]{1,2,0:T(8,128)} fusion(f32[1,128,8192]{1,2,0:T(8,128)} %copy.63, bf16[1,1,128,8192]{2,3,1,0:T(8,128)(2,1)} %copy.64), kind=kLoop, calls=%fused_computation.16 | loop fusion | flops 3145728 | bytes 10485760 | tf_op jit(solution)/shard_map/abs | solution.py:14
  61.4 2.9 reduce_max.38
  65.8 8.0 %all-to-all-start.3 = ((bf16[32,2,256]{2,1,0:T(2,128)(2,1)}), bf16[32,2,256]{2,1,0:T(2,128)(2,1)S(1)}, u32[]{:S(2)}, u32[]{:S(2)}) async-start(bf16[32,2,256]{2,1,0:T(2,128)(2,1)} %reshape.456), calls=%async_computation.3 | async-start | bytes 65536 | tf_op jit(solution)/shard_map/all_to_all | solution.py:30
  76.7 33.3 %copy.71 = bf16[1,1,128,8192]{2,1,0,3:T(2,128)(2,1)} copy(bf16[1,1,128,8192]{2,3,1,0:T(8,128)(2,1)S(1)} %fusion.5) | data formatting | bytes 4194304 | tf_op jit(solution)/shard_map/convert_element_type | solution.py:15
  110.0 45.2 %reduce.24 = bf16[8192,128]{1,0:T(8,128)(2,1)S(1)} reduce(bf16[8192,1,1,128]{3,2,1,0:T(2,128)(2,1)} %bitcast.129, bf16[]{:T(256)} %broadcast.212), dimensions={1,2}, to_apply=%bitcast.123.reduce_sub_computation | reduce | bytes 4194306
  157.3 7.9 %all-to-all-start = ((bf16[32,2,16384]{2,1,0:T(2,128)(2,1)}), bf16[32,2,16384]{2,1,0:T(2,128)(2,1)}, u32[]{:S(2)}, u32[]{:S(2)}) async-start(bf16[32,2,16384]{2,1,0:T(2,128)(2,1)} %reshape.458), calls=%async_computation | async-start | bytes 4194304 | tf_op jit(solution)/shard_map/all_to_all | solution.py:29
  168.1 33.3 %copy.70 = bf16[1,1,128,8192]{2,1,0,3:T(2,128)(2,1)} copy(bf16[1,1,128,8192]{2,3,1,0:T(8,128)(2,1)S(1)} %fusion.2) | data formatting | bytes 4194304 | tf_op jit(solution)/shard_map/convert_element_type | solution.py:15
  201.3 45.2 %reduce.22 = bf16[8192,128]{1,0:T(8,128)(2,1)S(1)} reduce(bf16[8192,1,1,128]{3,2,1,0:T(2,128)(2,1)} %bitcast.128, bf16[]{:T(256)} %broadcast.212), dimensions={1,2}, to_apply=%bitcast.122.reduce_sub_computation | reduce | bytes 4194306
  246.5 2.1 reshape.454
  248.7 7.4 %all-to-all-start.2 = ((bf16[32,2,16384]{2,1,0:T(2,128)(2,1)}), bf16[32,2,16384]{2,1,0:T(2,128)(2,1)S(1)}, u32[]{:S(2)}, u32[]{:S(2)}) async-start(bf16[32,2,16384]{2,1,0:T(2,128)(2,1)} %reshape.454), calls=%async_computation.2 | async-start | bytes 4194304 | tf_op jit(solution)/shard_map/all_to_all | solution.py:29
  256.7 10.5 %reshape.459 = bf16[8192,1,1,128]{3,2,1,0:T(2,128)(2,1)} reshape(bf16[32,2,16384]{2,1,0:T(2,128)(2,1)} %all-to-all-done) | data formatting | bytes 4194304
  267.1 7.0 %bitcast_convert_fusion = f32[1,1,128,8192]{2,1,0,3:T(1,128)S(1)} fusion(bf16[8192,1,1,128]{3,2,1,0:T(2,128)(2,1)} %reshape.459), kind=kLoop, calls=%fused_computation.49 | loop fusion | flops 1048576 | bytes 6291456 | tf_op jit(solution)/shard_map/convert_element_type | solution.py:20
  275.9 8.5 %all-to-all-done.2 = bf16[32,2,16384]{2,1,0:T(2,128)(2,1)S(1)} async-done(((bf16[32,2,16384]{2,1,0:T(2,128)(2,1)}), bf16[32,2,16384]{2,1,0:T(2,128)(2,1)S(1)}, u32[]{:S(2)}, u32[]{:S(2)}) %all-to-all-start.2) | async-done | bytes 2097184 | tf_op jit(solution)/shard_map/all_to_all | solution.py:29
  284.3 6.8 %reshape.455 = bf16[8192,1,1,128]{3,2,1,0:T(2,128)(2,1)} reshape(bf16[32,2,16384]{2,1,0:T(2,128)(2,1)S(1)} %all-to-all-done.2) | data formatting | bytes 4194304
  291.1 7.0 %bitcast_convert_fusion.1 = f32[1,1,128,8192]{2,1,0,3:T(1,128)S(1)} fusion(bf16[8192,1,1,128]{3,2,1,0:T(2,128)(2,1)} %reshape.455), kind=kLoop, calls=%fused_computation.50 | loop fusion | flops 1048576 | bytes 6291456 | tf_op jit(solution)/shard_map/convert_element_type | solution.py:20
  299.8 65.8 %all-reduce = (f32[1]{0:T(128)}, f32[1]{0:T(128)}) all-reduce(f32[1]{0:T(128)} %bitcast.32, f32[1]{0:T(128)} %bitcast.11), channel_id=1, replica_groups=mesh['replica'=32,'fsdp'=4] {'replica','fsdp'}, use_global_device_ids=true, to_apply=%region_8.0 | all-reduce | flops 2 | bytes 16 | tf_op jit(solution)/shard_map/psum | solution.py:35
  369.4 22.3 %all-gather.2 = bf16[32,4,128]{2,1,0:T(4,128)(2,1)S(1)} all-gather(bf16[1,4,128]{2,1,0:T(4,128)(2,1)S(1)} %get-tuple-element.26), channel_id=2, replica_groups=mesh['replica'=32,'fsdp'=4] {'replica'}, dimensions={0}, use_global_device_ids=true | all-gather | bytes 33792 | tf_op jit(solution)/shard_map/all_gather | solution.py:46
  391.6 23.9 %all-gather.3 = bf16[32,4,128]{2,1,0:T(4,128)(2,1)S(1)} all-gather(bf16[1,4,128]{2,1,0:T(4,128)(2,1)S(1)} %get-tuple-element.28), channel_id=3, replica_groups=mesh['replica'=32,'fsdp'=4] {'replica'}, dimensions={0}, use_global_device_ids=true | all-gather | bytes 33792 | tf_op jit(solution)/shard_map/all_gather | solution.py:46
  415.6 5.3 %fusion.4 = f32[1,128,8192]{1,2,0:T(8,128)} fusion(f32[1,128,8192]{1,2,0:T(8,128)} %copy.60, bf16[1,128,8192]{1,2,0:T(8,128)(2,1)} %all-gather.7.cloned.1.call-done, f32[128,128]{0,1:T(8,128)S(1)} %convert_bitcast_fusion.2), kind=kLoop, calls=%fused_computation.10 | loop fusion | flops 4194304 | bytes 10551296 | tf_op jit(solution)/shard_map/sub | solution.py:48
  420.9 32.9 %all-gather.9.cloned.1.call-done = bf16[1,128,8192]{1,2,0:T(8,128)(2,1)} async-done(((bf16[1,128,256]{1,2,0:T(8,128)(2,1)}), bf16[1,128,8192]{1,2,0:T(8,128)(2,1)}) %all-gather.9.cloned.1.call-update) | async-done | bytes 2097168 | tf_op jit(solution)/shard_map/all_gather | solution.py:45
  453.8 3.5 fusion.1
  457.9 3.8 pad_maximum_fusion
  461.7 8.9 %copy.56 = f32[2,128,8192]{2,1,0:T(8,128)} copy(f32[2,128,8192]{1,2,0:T(8,128)} %pad_maximum_fusion) | data formatting | bytes 16777216
  (58 shorter events, 18.2 us)
Async XLA Ops:
  37.9 27.9 %all-to-all-start.1 = ((bf16[32,2,256]{2,1,0:T(2,128)(2,1)}), bf16[32,2,256]{2,1,0:T(2,128)(2,1)S(1)}, u32[]{:S(2)}, u32[]{:S(2)}) async-start(bf16[32,2,256]{2,1,0:T(2,128)(2,1)} %reshape.460), calls=%async_computation.1 | async-start | bytes 65536 | tf_op jit(solution)/shard_map/all_to_all | solution.py:30
  65.8 91.4 %all-to-all-start.3 = ((bf16[32,2,256]{2,1,0:T(2,128)(2,1)}), bf16[32,2,256]{2,1,0:T(2,128)(2,1)S(1)}, u32[]{:S(2)}, u32[]{:S(2)}) async-start(bf16[32,2,256]{2,1,0:T(2,128)(2,1)} %reshape.456), calls=%async_computation.3 | async-start | bytes 65536 | tf_op jit(solution)/shard_map/all_to_all | solution.py:30
  73.8 2.2 copy-start
  157.2 8.2 %copy-start.2 = (bf16[1,1,128,8192]{2,3,1,0:T(8,128)(2,1)S(1)}, bf16[1,1,128,8192]{2,3,1,0:T(8,128)(2,1)}, u32[]{:S(2)}) copy-start(bf16[1,1,128,8192]{2,3,1,0:T(8,128)(2,1)} %copy.64) | copy-start | bytes 6291460
  157.3 91.4 %all-to-all-start = ((bf16[32,2,16384]{2,1,0:T(2,128)(2,1)}), bf16[32,2,16384]{2,1,0:T(2,128)(2,1)}, u32[]{:S(2)}, u32[]{:S(2)}) async-start(bf16[32,2,16384]{2,1,0:T(2,128)(2,1)} %reshape.458), calls=%async_computation | async-start | bytes 4194304 | tf_op jit(solution)/shard_map/all_to_all | solution.py:29
  165.2 2.2 copy-start.1
  246.5 9.8 %copy-start.4 = (f32[2,128,256]{2,1,0:T(8,128)S(1)}, f32[2,128,256]{2,1,0:T(8,128)}, u32[]{:S(2)}) copy-start(f32[2,128,256]{2,1,0:T(8,128)} %param.5) | copy-start | bytes 786436
  248.7 35.7 %all-to-all-start.2 = ((bf16[32,2,16384]{2,1,0:T(2,128)(2,1)}), bf16[32,2,16384]{2,1,0:T(2,128)(2,1)S(1)}, u32[]{:S(2)}, u32[]{:S(2)}) async-start(bf16[32,2,16384]{2,1,0:T(2,128)(2,1)} %reshape.454), calls=%async_computation.2 | async-start | bytes 4194304 | tf_op jit(solution)/shard_map/all_to_all | solution.py:29
  256.0 159.6 %all-gather.7.cloned.1.call-start = ((), (), s32[]{:S(2)}) async-start(), calls=%async_computation.4 | async-start | bytes 2162688 | tf_op jit(solution)/shard_map/all_gather | solution.py:45
  367.7 86.1 %all-gather.9.cloned.1.call-start = ((), (), s32[]{:S(2)}) async-start(), calls=%async_computation.5 | async-start | bytes 2162688 | tf_op jit(solution)/shard_map/all_gather | solution.py:45
  453.8 4.1 copy-start.3
Sparse Core Ops, SparseCore 0:
  367.9 40.5 all-gather.6
  410.7 43.1 all-gather.8
where the time goes:
time: 484 us; the launch traced here: 478 us
  other arithmetic  140 us (29%)
  local copies, waits for them, and re-layouts  136 us (28%)
  blocking collectives  112 us (23%)
  waiting for transfers between devices  41.4 us (9%)
  starting transfers between devices  32.2 us (7%)
  between operations  16 us (3%)
    unnamed x6, other arithmetic  92 us
    convert_element_type x2, local copies, waits for them, and re-layouts, quantize(): (blocks / scales.astype(jnp.float32)[..., None]).astype(jnp.bfloat16)  66.6 us
    psum x1, blocking collectives, synchronize(): norm_squared = lax.psum(squares, ('replica', 'fsdp'))  65.8 us
    unnamed x27, local copies, waits for them, and re-layouts  56 us
    all_gather x2, blocking collectives, synchronize(): lax.all_gather(step_scales, 'replica', axis=2, tiled=True)  46.2 us
    all_gather x2, waiting for transfers between devices, synchronize(): lax.all_gather(step_codes, 'replica', axis=2, tiled=True)  32.9 us
    all_to_all x2, starting transfers between devices, synchronize(): lax.all_to_all(block_scales[None], 'replica', split_axis=3, concat_axis=0...  16.5 us
    all_to_all x2, starting transfers between devices, synchronize(): lax.all_to_all(block_codes[None], 'replica', split_axis=3, concat_axis=0,...  15.3 us
  transfers between devices with their start and end apart: 6, of which 2 were waited for; matrix products, arithmetic and copies ran while one was open for 44% of the time, Pallas kernels for 0%

commit v1 on v0

v1 whole, which is shorter than its diff:
```python
import functools

import jax
import jax.numpy as jnp
from jax import lax
from jax.experimental import pallas as pl
from jax.experimental.pallas import tpu as pltpu
from jax.sharding import PartitionSpec as P

OUTER_MOMENTUM = 0.9
OUTER_RATE = 0.7
CLIP_LEVEL = 1.0
MESH = pl.DeviceIdType.MESH
RING = 4
F32, BF16 = jnp.float32, jnp.bfloat16


def kernel(zs, count, copies, lw_hbm, gw_hbm, mom_hbm, out_hbm, mout_hbm,
           gw, lw, mom, mout, ds, dr, s_send, s_mid, s_end, tt, t_send, t_mid, t_end, av, n1, n2, g, h,
           in_sems, out_sems, mom_sems, send_sems, recv_sems, norm_send, norm_recv):
    frags, rows, _ = gw.shape
    width = mom.shape[2]
    half_rows, quarter = rows // 2, rows // 4
    r = lax.axis_index("replica")
    z = lax.axis_index("fsdp")
    core = r % 2
    y = (r // 2) % RING
    x = r // (2 * RING)

    def dev(ox, oy, oc=0, oz=0):
        ax, ay = (x + ox) % RING, (y + oy) % RING
        return ((ax * RING + ay) * 2 + (core + oc) % 2, (z + oz) % zs)

    def along(axis, o):
        return dev(o, 0) if axis == 0 else dev(0, o)

    def column(first, o, j, c):
        ax, ay = (x + (o if first == 0 else j)) % RING, (y + (j if first == 0 else o)) % RING
        return pl.multiple_of(((ax * RING + ay) * 2 + c) * width, width)

    started = []

    def send(src, dst, device):
        i = len(started)
        copy = pltpu.make_async_remote_copy(
            src_ref=src, dst_ref=dst, send_sem=send_sems.at[i], recv_sem=recv_sems.at[i],
            device_id=device, device_id_type=MESH)
        copy.start()
        started.append(copy)
        return copy

    loads = {}
    for f in range(frags):
        for hf in range(2):
            at = pl.ds(hf * half_rows, half_rows)
            loads[f, hf] = [
                pltpu.make_async_copy(gw_hbm.at[f, at], gw.at[f, at], in_sems.at[f, hf, 0]),
                pltpu.make_async_copy(lw_hbm.at[0, f, at], lw.at[f, at], in_sems.at[f, hf, 1])]
            for copy in loads[f, hf]:
                copy.start()
    mom_load = pltpu.make_async_copy(mom_hbm, mom, mom_sems.at[0])
    mom_load.start()

    near = [(0, 0, oc, oz) for oz in range(zs) for oc in range(2) if (oc, oz) != (0, 0)]
    far = [(ox, oy, 0, 0) for ox in range(RING) for oy in range(RING) if (ox, oy) != (0, 0)]
    barrier = pltpu.get_barrier_semaphore()
    for partner in near + far:
        pl.semaphore_signal(barrier, inc=1, device_id=dev(*partner), device_id_type=MESH)
    pl.semaphore_wait(barrier, len(near) + len(far))

    def difference(f, row, n, col):
        at = pl.ds(row, n)
        return gw[f, at, pl.ds(col, width)] - lw[f, at, pl.ds(col, width)].astype(F32)

    core_copies, mid, end, mid2, end2 = {}, {}, {}, {}, {}

    def to_core(f, hf):
        for copy in loads[f, hf]:
            copy.wait()
        for o in (2, 1, 3, 0):
            @pl.loop(0, RING)
            def _(j):
                col = column(hf, o, j, 1 - core)
                ds[f, hf, o, j] = difference(f, hf * half_rows, half_rows, col).astype(BF16)
            core_copies[f, hf, o] = send(ds.at[f, hf, o], dr.at[f, hf, o], dev(0, 0, 1))

    def pair_sum(f, hf, o, j, q, n):
        col = column(hf, o, j, core)
        return (difference(f, hf * half_rows + q * quarter, n * quarter, col)
                + dr[f, hf, o, j, pl.ds(q * quarter, n * quarter)].astype(F32))

    def ring1_open(f, hf):
        core_copies[f, hf, 2].wait_recv()
        for q in range(2):
            @pl.loop(0, RING)
            def _(j):
                s_send[f, hf, 1, q, j] = pair_sum(f, hf, 2, j, q, 1).astype(BF16)
            mid[f, hf, q] = send(s_send.at[f, hf, 1, q], s_mid.at[f, hf, q], along(hf, 1 if q == 0 else -1))
        for o, q, way in ((1, 1, 1), (3, 0, -1)):
            core_copies[f, hf, o].wait_recv()

            @pl.loop(0, RING)
            def _(j):
                s_send[f, hf, o - 1, q, j] = pair_sum(f, hf, o, j, q, 1).astype(BF16)
            k = 0 if way == 1 else 1
            end[f, hf, k, q] = send(s_send.at[f, hf, o - 1, q], s_end.at[f, hf, k, q], along(hf, way))

    def ring1_middle(f, hf):
        for o, q, way in ((1, 0, 1), (3, 1, -1)):
            mid[f, hf, q].wait_recv()

            @pl.loop(0, RING)
            def _(j):
                total = pair_sum(f, hf, o, j, q, 1) + s_mid[f, hf, q, j].astype(F32)
                s_send[f, hf, o - 1, q, j] = total.astype(BF16)
            k = 0 if way == 1 else 1
            end[f, hf, k, q] = send(s_send.at[f, hf, o - 1, q], s_end.at[f, hf, k, q], along(hf, way))

    def ring2_open(f, hf):
        core_copies[f, hf, 0].wait_recv()
        for k in range(2):
            for q in range(2):
                end[f, hf, k, q].wait_recv()

        def whole(j):
            for q in range(2):
                total = pair_sum(f, hf, 0, j, q, 1)
                total = total + s_end[f, hf, 0, q, j].astype(F32) + s_end[f, hf, 1, q, j].astype(F32)
                tt[f, hf, j, q] = total
                if j:
                    t_send[f, hf, j - 1, q] = total.astype(BF16)

        whole(2)
        for q in range(2):
            mid2[f, hf, q] = send(t_send.at[f, hf, 1, q], t_mid.at[f, hf, q], along(1 - hf, 1 if q == 0 else -1))
        whole(1)
        end2[f, hf, 0, 1] = send(t_send.at[f, hf, 0, 1], t_end.at[f, hf, 0, 1], along(1 - hf, 1))
        whole(3)
        end2[f, hf, 1, 0] = send(t_send.at[f, hf, 2, 0], t_end.at[f, hf, 1, 0], along(1 - hf, -1))
        whole(0)

    def ring2_middle(f, hf):
        for j, q, way in ((1, 0, 1), (3, 1, -1)):
            mid2[f, hf, q].wait_recv()
            t_send[f, hf, j - 1, q] = (tt[f, hf, j, q] + t_mid[f, hf, q].astype(F32)).astype(BF16)
            k = 0 if way == 1 else 1
            end2[f, hf, k, q] = send(t_send.at[f, hf, j - 1, q], t_end.at[f, hf, k, q], along(1 - hf, way))

    def ring2_close(f, hf):
        total = 0.0
        for q in range(2):
            for k in range(2):
                end2[f, hf, k, q].wait_recv()
            part = tt[f, hf, 0, q] + t_end[f, hf, 0, q].astype(F32) + t_end[f, hf, 1, q].astype(F32)
            part = part * (1.0 / (2 * RING * RING))
            av[f, pl.ds(hf * half_rows + q * quarter, quarter)] = part
            square = jnp.sum((part * part).reshape(quarter // 8, 8, width), axis=0)
            for c in range(width // 128):
                total = total + square[:, c * 128:(c + 1) * 128]
        return total

    def exchange(f, stage, tiles, partners):
        n = len(partners)
        for i, partner in enumerate(partners):
            pltpu.make_async_remote_copy(
                src_ref=tiles.at[f, n], dst_ref=tiles.at[f, i], send_sem=norm_send.at[f, stage],
                recv_sem=norm_recv.at[f, stage], device_id=dev(*partner), device_id_type=MESH).start()

    def gathered(f, stage, tiles, partners):
        part = tiles.at[f, pl.ds(0, len(partners))]
        pltpu.make_async_copy(part, part, norm_recv.at[f, stage]).wait()
        return jnp.sum(tiles[f], axis=0)

    def norm_open(f, total):
        n1[f, len(near)] = total
        exchange(f, 0, n1, near)

    def norm_middle(f):
        n2[f, len(far)] = gathered(f, 0, n1, near)
        exchange(f, 1, n2, far)

    gathers = {}
    mom_stores = {}

    def outer(f):
        total = gathered(f, 1, n2, far)
        norm_squared = jnp.sum(total, axis=(0, 1), keepdims=True)
        factor = jnp.minimum(1.0, CLIP_LEVEL * jnp.sqrt(F32(count)) / jnp.sqrt(norm_squared + 1e-06))
        for hf in range(2):
            at = pl.ds(hf * half_rows, half_rows)
            clipped = av[f, at] * factor
            moment = OUTER_MOMENTUM * mom[f, at] + clipped
            mout[f, at] = moment
            g[f, hf, 0, 0] = (clipped + OUTER_MOMENTUM * moment).astype(BF16)
            for way in (1, -1):
                pass_on(f, hf, 1, 0, 0, way, None)
            for way in (1, -1):
                pass_on(f, hf, 2, 0, 0, way, None)
        mom_stores[f] = pltpu.make_async_copy(mout.at[f], mout_hbm.at[f], mom_sems.at[1 + f])
        mom_stores[f].start()

    def pass_on(f, hf, ring, o2, o1, way, q):
        axis = 1 - hf if ring == 1 else hf
        to2, to1 = (o2, (o1 - way) % RING) if ring == 1 else ((o2 - way) % RING, o1)
        src, dst = g.at[f, hf, o2, o1], g.at[f, hf, to2, to1]
        if q is not None:
            at = pl.ds(q * quarter, quarter)
            src, dst = src.at[at], dst.at[at]
        gathers[f, hf, to2, to1, q] = send(src, dst, along(axis, way))

    def arrived(f, hf, o2, o1):
        for q in (0, 1) if (o2 == 2 if o2 else o1 == 2) else (None,):
            gathers[f, hf, o2, o1, q].wait_recv()

    def gather1_middle(f, hf):
        for o1, way, q in ((3, 1, 0), (1, -1, 1)):
            arrived(f, hf, 0, o1)
            pass_on(f, hf, 1, 0, o1, way, q)
            for way2 in (1, -1):
                pass_on(f, hf, 2, 0, o1, way2, None)

    def gather1_close(f, hf):
        arrived(f, hf, 0, 2)
        for way in (1, -1):
            pass_on(f, hf, 2, 0, 2, way, None)
        hand_over(f, hf, 0)

    def gather2_middle(f, hf):
        for o1 in (0, 3, 1, 2):
            for o2, way, q in ((3, 1, 0), (1, -1, 1)):
                arrived(f, hf, o2, o1)
                pass_on(f, hf, 2, o2, o1, way, q)
        for o2 in (3, 1):
            hand_over(f, hf, o2)

    def gather2_close(f, hf):
        for o1 in range(RING):
            arrived(f, hf, 2, o1)
        hand_over(f, hf, 2)

    handed = {}

    def hand_over(f, hf, o2):
        handed[f, hf, o2] = send(g.at[f, hf, o2], h.at[f, hf, o2], dev(0, 0, 1))

    def refresh(f, hf, o2, blocks, c):
        at = pl.ds(hf * half_rows, half_rows)

        @pl.loop(0, RING)
        def _(j):
            col = pl.ds(column(hf, o2, j, c), width)
            gw[f, at, col] = gw[f, at, col] - OUTER_RATE * blocks[f, hf, o2, j].astype(F32)

    stores = []

    def store(f, hf, o2):
        at = pl.ds(hf * half_rows, half_rows)
        if hf == 0:
            n = RING * 2 * width
            cols = [pl.ds(pl.multiple_of(((x + o2) % RING) * n, n), n)]
        else:
            n = 2 * width
            cols = [pl.ds(pl.multiple_of((ax * RING + (y + o2) % RING) * n, n), n) for ax in range(RING)]
        for i, col in enumerate(cols):
            copy = pltpu.make_async_copy(gw.at[f, at, col], out_hbm.at[f, at, col], out_sems.at[f, hf, o2, i])
            copy.start()
            stores.append(copy)

    def own(f, hf, o2):
        refresh(f, hf, o2, g, core)

    def other(f, hf, o2):
        handed[f, hf, o2].wait_recv()
        refresh(f, hf, o2, h, 1 - core)
        store(f, hf, o2)

    both = range(2)
    for hf in both:
        to_core(0, hf)
    for hf in both:
        ring1_open(0, hf)
    for hf in both:
        to_core(1, hf)
    for hf in both:
        ring1_middle(0, hf)
    for hf in both:
        ring1_open(1, hf)
    for hf in both:
        ring2_open(0, hf)
    for hf in both:
        ring2_middle(0, hf)
    for hf in both:
        ring1_middle(1, hf)
    norm_open(0, ring2_close(0, 0) + ring2_close(0, 1))
    for hf in both:
        ring2_open(1, hf)
    norm_middle(0)
    for hf in both:
        ring2_middle(1, hf)
    mom_load.wait()
    outer(0)
    norm_open(1, ring2_close(1, 0) + ring2_close(1, 1))
    for hf in both:
        gather1_middle(0, hf)
    norm_middle(1)
    for hf in both:
        gather1_close(0, hf)
    outer(1)
    for hf in both:
        gather2_middle(0, hf)
    for hf in both:
        gather1_middle(1, hf)
    for hf in both:
        gather1_close(1, hf)
    for hf in both:
        gather2_close(0, hf)
    for o2 in (0, 3, 1, 2):
        for hf in both:
            own(0, hf, o2)
            other(0, hf, o2)
    for hf in both:
        gather2_middle(1, hf)
    for hf in both:
        for o2 in (0, 3, 1):
            own(1, hf, o2)
            other(1, hf, o2)
    for hf in both:
        gather2_close(1, hf)
    for hf in both:
        own(1, hf, 2)
    for hf in both:
        other(1, hf, 2)

    assert len(started) == copies, len(started)
    for copy in started:
        copy.wait_send()
    for f in range(frags):
        for stage, tiles, n in ((0, n1, len(near)), (1, n2, len(far))):
            part = tiles.at[f, pl.ds(0, n)]
            pltpu.make_async_copy(part, part, norm_send.at[f, stage]).wait()
        mom_stores[f].wait()
    for copy in stores:
        copy.wait()


COPIES = 160


def synchronize(local_weights, global_weights, momentum):
    frags, rows, cols = global_weights.shape
    width = momentum.shape[2]
    zs = lax.axis_size("fsdp")
    assert lax.axis_size("replica") == 2 * RING * RING and frags == 2
    half_rows, quarter = rows // 2, rows // 4
    vmem = lambda shape, dtype: pltpu.VMEM(shape, dtype)
    anywhere = pl.BlockSpec(memory_space=pl.ANY)
    return pl.pallas_call(
        functools.partial(kernel, zs, rows * zs * cols, COPIES),
        out_shape=(
            jax.ShapeDtypeStruct(global_weights.shape, F32),
            jax.ShapeDtypeStruct(momentum.shape, F32),
        ),
        in_specs=[anywhere] * 3,
        out_specs=(anywhere, anywhere),
        scratch_shapes=[
            vmem((frags, rows, cols), F32),
            vmem((frags, rows, cols), BF16),
            vmem((frags, rows, width), F32),
            vmem((frags, rows, width), F32),
            vmem((frags, 2, RING, RING, half_rows, width), BF16),
            vmem((frags, 2, RING, RING, half_rows, width), BF16),
            vmem((frags, 2, RING - 1, 2, RING, quarter, width), BF16),
            vmem((frags, 2, 2, RING, quarter, width), BF16),
            vmem((frags, 2, 2, 2, RING, quarter, width), BF16),
            vmem((frags, 2, RING, 2, quarter, width), F32),
            vmem((frags, 2, RING - 1, 2, quarter, width), BF16),
            vmem((frags, 2, 2, quarter, width), BF16),
            vmem((frags, 2, 2, 2, quarter, width), BF16),
            vmem((frags, rows, width), F32),
            vmem((frags, 2 * zs, 8, 128), F32),
            vmem((frags, RING * RING, 8, 128), F32),
            vmem((frags, 2, RING, RING, half_rows, width), BF16),
            vmem((frags, 2, RING, RING, half_rows, width), BF16),
            pltpu.SemaphoreType.DMA((frags, 2, 2)),
            pltpu.SemaphoreType.DMA((frags, 2, RING, RING)),
            pltpu.SemaphoreType.DMA((1 + frags,)),
            pltpu.SemaphoreType.DMA((COPIES,)),
            pltpu.SemaphoreType.DMA((COPIES,)),
            pltpu.SemaphoreType.DMA((frags, 2)),
            pltpu.SemaphoreType.DMA((frags, 2)),
        ],
        compiler_params=pltpu.CompilerParams(
            collective_id=0, has_side_effects=True, vmem_limit_bytes=48 * 2**20
        ),
        cost_estimate=pl.CostEstimate(flops=20 * rows * cols, bytes_accessed=20 * frags * rows * cols // 2, transcendentals=0),
    )(local_weights, global_weights, momentum)


def solution(mesh):
    return jax.shard_map(
        synchronize,
        mesh=mesh,
        in_specs=(
            P("replica", None, "fsdp", None),
            P(None, "fsdp", None),
            P(None, "fsdp", "replica"),
        ),
        out_specs=(P(None, "fsdp", None), P(None, "fsdp", "replica")),
        check_vma=False,
    )
```

time: 484 us -> 76.3 us (0.16); the launches traced: 478 us -> 76.1 us
  other arithmetic: 140 us -> 0 us
  local copies, waits for them, and re-layouts: 136 us -> 11.5 us
  blocking collectives: 112 us -> 0 us
  Pallas kernels: 0 us -> 63.9 us
  waiting for transfers between devices: 41.4 us -> 0 us
  starting transfers between devices: 32.2 us -> 0 us
  between operations: 16 us -> 0.65 us
    unnamed x6 -> x0, other arithmetic: 92 us -> none
    convert_element_type x4 -> x0, local copies, waits for them, and re-layouts: 66.7 us -> none  [the longest x2 66.6 us: quantize(): (blocks / scales.astype(jnp.float32)[..., None]).astype(jnp.bfloat16)]
    psum x1 -> x0, blocking collectives: 65.8 us -> none  [synchronize(): norm_squared = lax.psum(squares, ('replica', 'fsdp'))]
    pallas_call x0 -> x1, Pallas kernels: none -> 63.9 us  [synchronize(): pl.pallas_call(functools.partial(kernel, zs, rows * zs * cols, COPIES), o...]
    all_gather x2 -> x0, blocking collectives: 46.2 us -> none  [synchronize(): lax.all_gather(step_scales, 'replica', axis=2, tiled=True)]
    unnamed x27 -> x6, local copies, waits for them, and re-layouts: 56 us -> 11.5 us
    all_gather x2 -> x0, waiting for transfers between devices: 32.9 us -> none  [synchronize(): lax.all_gather(step_codes, 'replica', axis=2, tiled=True)]
    all_to_all x4 -> x0, starting transfers between devices: 31.9 us -> none  [the longest x2 16.5 us: synchronize(): lax.all_to_all(block_scales[None], 'replica', split_axis=3, concat_axis=0...]
  transfers between devices with their start and end apart: 6 -> 0, of which waited for: 2 -> 0; matrix products, arithmetic and copies ran while one was open for 44% -> 0% of each run, Pallas kernels for 0% -> 0%
where the time goes in v1:
time: 76.3 us; the launch traced here: 76.1 us
  Pallas kernels  63.9 us (84%)
  local copies, waits for them, and re-layouts  11.5 us (15%)
    pallas_call x1, Pallas kernels, synchronize(): pl.pallas_call(functools.partial(kernel, zs, rows * zs * cols, COPIES), o...  63.9 us
    unnamed x6, local copies, waits for them, and re-layouts  11.5 us

profile of v1, /device:TPU:1, one launch (start us, length us, event | category | flops | bytes accessed | tf_op | source)
XLA Modules:
  0.0 76.1 jit_solution(5665290828716593883)
XLA Ops:
  0.6 0.0 copy-start
  0.6 2.2 %copy-done = bf16[1,2,128,8192]{3,2,1,0:T(8,128)(2,1)S(1)} copy-done((bf16[1,2,128,8192]{3,2,1,0:T(8,128)(2,1)S(1)}, bf16[1,2,128,8192]{3,2,1,0:T(8,128)(2,1)}, u32[]{:S(2)}) %copy-start) | copy-done | bytes 4194328
  2.8 0.0 copy-start.1
  2.8 0.9 %copy-done.1 = f32[2,128,256]{2,1,0:T(8,128)S(1)} copy-done((f32[2,128,256]{2,1,0:T(8,128)S(1)}, f32[2,128,256]{2,1,0:T(8,128)}, u32[]{:S(2)}) %copy-start.1) | copy-done | bytes 262168
  3.8 63.9 %shard_map.50 = (f32[2,128,8192]{2,1,0:T(8,128)}, f32[2,128,256]{2,1,0:T(8,128)S(1)}) custom-call(bf16[1,2,128,8192]{3,2,1,0:T(8,128)(2,1)S(1)} %copy-done, f32[2,128,8192]{2,1,0:T(8,128)} %gw_hbm.1, f32[2,128,256]{2,1,0:T(8,128)S(1)} %copy-done.1), custom_call_target="tpu_custom_call" | custom-call | flops 20971520 | bytes 20971520 | tf_op jit(solution)/shard_map/pallas_call | solution.py:357
  67.7 7.7 %copy.7 = f32[2,128,8192]{2,1,0:T(8,128)} copy(f32[2,128,8192]{2,1,0:T(8,128)} %get-tuple-element.4) | data formatting | bytes 16777216
  75.4 0.7 copy.8
Async XLA Ops:
  0.6 2.2 %copy-start = (bf16[1,2,128,8192]{3,2,1,0:T(8,128)(2,1)S(1)}, bf16[1,2,128,8192]{3,2,1,0:T(8,128)(2,1)}, u32[]{:S(2)}) copy-start(bf16[1,2,128,8192]{3,2,1,0:T(8,128)(2,1)} %lw_hbm.1) | copy-start | bytes 12582916
  2.8 0.9 %copy-start.1 = (f32[2,128,256]{2,1,0:T(8,128)S(1)}, f32[2,128,256]{2,1,0:T(8,128)}, u32[]{:S(2)}) copy-start(f32[2,128,256]{2,1,0:T(8,128)} %mom_hbm.1) | copy-start | bytes 786436

commit v2 on v0

v2 whole, which is shorter than its diff:
```python
import functools

import jax
import jax.numpy as jnp
from jax import lax
from jax.experimental import pallas as pl
from jax.experimental.pallas import tpu as pltpu
from jax.sharding import PartitionSpec as P

OUTER_MOMENTUM = 0.9
OUTER_RATE = 0.7
CLIP_LEVEL = 1.0
MESH = pl.DeviceIdType.MESH
RING = 4
OFFSETS = (0, 1, -1, 2)
F32, BF16 = jnp.float32, jnp.bfloat16


def kernel(zs, count, lw_hbm, gw_hbm, mom_hbm, gw, mout,
           lw, mom, ds, dr, s_send, s_mid, s_end, tt, t_send, t_end, av, n1, n2, g, h,
           in_sems, send_sems, norm_sems, core_sems, mid_sems, end_sems, end2_sems, gather_sems, hand_sems):
    frags, rows, _ = gw.shape
    width = mom.shape[2]
    half_rows, quarter = rows // 2, rows // 4
    r = lax.axis_index("replica")
    z = lax.axis_index("fsdp")
    core = r % 2
    y = (r // 2) % RING
    x = r // (2 * RING)
    both = range(2)

    def dev(ox, oy, oc=0, oz=0):
        ax, ay = (x + ox) % RING, (y + oy) % RING
        return ((ax * RING + ay) * 2 + (core + oc) % 2, (z + oz) % zs)

    def along(axis, o):
        return dev(o, 0) if axis == 0 else dev(0, o)

    def column(hf, a, b, c):
        ax, ay = (x + (a if hf == 0 else b)) % RING, (y + (b if hf == 0 else a)) % RING
        return pl.multiple_of(((ax * RING + ay) * 2 + c) * width, width)

    def offset(slot):
        return jnp.where(slot == 2, -1, jnp.where(slot == 3, 2, slot))

    def send(src, dst, family, recv_sem, device):
        pltpu.make_async_remote_copy(
            src_ref=src, dst_ref=dst, send_sem=send_sems.at[family], recv_sem=recv_sem,
            device_id=device, device_id_type=MESH).start()

    def wait(ref, sem):
        pltpu.make_async_copy(ref, ref, sem).wait()

    loads = {}
    for f in range(frags):
        for hf in both:
            at = pl.ds(hf * half_rows, half_rows)
            loads[f, hf] = [
                pltpu.make_async_copy(gw_hbm.at[f, at], gw.at[f, at], in_sems.at[f, hf, 0]),
                pltpu.make_async_copy(lw_hbm.at[0, f, at], lw.at[f, at], in_sems.at[f, hf, 1])]

    def start_loads(f):
        for hf in both:
            for copy in loads[f, hf]:
                copy.start()

    start_loads(0)

    near = [(0, 0, oc, oz) for oz in range(zs) for oc in range(2) if (oc, oz) != (0, 0)]
    far = [(ox, oy, 0, 0) for ox in range(RING) for oy in range(RING) if (ox, oy) != (0, 0)]
    greeted = near + [(1, 0, 0, 0), (-1, 0, 0, 0), (0, 1, 0, 0), (0, -1, 0, 0)]
    barrier = pltpu.get_barrier_semaphore()
    for partner in greeted:
        pl.semaphore_signal(barrier, inc=1, device_id=dev(*partner), device_id_type=MESH)
    pl.semaphore_wait(barrier, len(greeted))

    start_loads(1)
    mom_load = pltpu.make_async_copy(mom_hbm, mom, in_sems.at[0, 0, 2])
    mom_load.start()

    def difference(f, row, n, col):
        at = pl.ds(row, n)
        return gw[f, at, pl.ds(col, width)] - lw[f, at, pl.ds(col, width)].astype(F32)

    def load(f, hf):
        for copy in loads[f, hf]:
            copy.wait()

    def to_core(f, slot, hf):
        @pl.loop(0, RING)
        def _(j):
            col = column(hf, OFFSETS[slot], offset(j), 1 - core)
            ds[f, slot, hf, j] = difference(f, hf * half_rows, half_rows, col).astype(BF16)
        send(ds.at[f, slot, hf], dr.at[f, slot, hf], 0, core_sems.at[f, slot], dev(0, 0, 1))

    def from_core(f, slot):
        wait(dr.at[f, slot], core_sems.at[f, slot])

    def pair_sum(f, hf, slot, j, row, n):
        col = column(hf, OFFSETS[slot], offset(j), core)
        return (difference(f, hf * half_rows + row, n, col)
                + dr[f, slot, hf, j, pl.ds(row, n)].astype(F32))

    def ring1_far(f, hf):
        for q, way in ((0, 1), (1, -1)):
            @pl.loop(0, RING)
            def _(j):
                s_send[f, hf, 2, q, j] = pair_sum(f, hf, 3, j, q * quarter, quarter).astype(BF16)
            send(s_send.at[f, hf, 2, q], s_mid.at[f, hf, q], 1, mid_sems.at[f, hf], along(hf, way))

    def ring1_near(f, hf, slot):
        q, way = (1, 1) if slot == 1 else (0, -1)

        @pl.loop(0, RING)
        def _(j):
            s_send[f, hf, slot - 1, q, j] = pair_sum(f, hf, slot, j, q * quarter, quarter).astype(BF16)
        send(s_send.at[f, hf, slot - 1, q], s_end.at[f, hf, slot - 1, q], 1, end_sems.at[f, hf], along(hf, way))

    def ring1_middle(f, hf):
        wait(s_mid.at[f, hf], mid_sems.at[f, hf])
        for slot, q, way in ((1, 0, 1), (2, 1, -1)):
            @pl.loop(0, RING)
            def _(j):
                total = pair_sum(f, hf, slot, j, q * quarter, quarter) + s_mid[f, hf, q, j].astype(F32)
                s_send[f, hf, slot - 1, q, j] = total.astype(BF16)
            send(s_send.at[f, hf, slot - 1, q], s_end.at[f, hf, slot - 1, q], 1, end_sems.at[f, hf], along(hf, way))

    def ring2_open(f, hf):
        wait(s_end.at[f, hf], end_sems.at[f, hf])

        def whole(j, q):
            total = pair_sum(f, hf, 0, j, q * quarter, quarter)
            return total + s_end[f, hf, 0, q, j].astype(F32) + s_end[f, hf, 1, q, j].astype(F32)

        for slot in (3, 1, 2):
            for q in both:
                t_send[f, hf, slot - 1, pl.ds(q * quarter, quarter)] = whole(slot, q).astype(BF16)
            send(t_send.at[f, hf, slot - 1], t_end.at[f, hf, slot - 1], 2, end2_sems.at[f, hf],
                 along(1 - hf, OFFSETS[slot]))
        for q in both:
            tt[f, hf, pl.ds(q * quarter, quarter)] = whole(0, q)

    def ring2_close(f, hf):
        wait(t_end.at[f, hf], end2_sems.at[f, hf])
        part = tt[f, hf]
        for k in range(RING - 1):
            part = part + t_end[f, hf, k].astype(F32)
        part = part * (1.0 / (2 * RING * RING))
        av[f, pl.ds(hf * half_rows, half_rows)] = part
        square = jnp.sum((part * part).reshape(half_rows // 8, 8, width), axis=0)
        total = square[:, :128]
        for c in range(1, width // 128):
            total = total + square[:, c * 128:(c + 1) * 128]
        return total

    def exchange(f, stage, tiles, partners):
        n = len(partners)
        for i, partner in enumerate(partners):
            send(tiles.at[f, n], tiles.at[f, i], 3 + stage, norm_sems.at[f, stage], dev(*partner))

    def gathered(f, stage, tiles, partners):
        wait(tiles.at[f, pl.ds(0, len(partners))], norm_sems.at[f, stage])
        return jnp.sum(tiles[f], axis=0)

    def norm_open(f):
        n1[f, len(near)] = ring2_close(f, 0) + ring2_close(f, 1)
        exchange(f, 0, n1, near)

    def norm_middle(f):
        n2[f, len(far)] = gathered(f, 0, n1, near)
        exchange(f, 1, n2, far)

    def gather1(f, hf, slot, family, k):
        back = (None, 2, 1, 3)[slot]
        send(g.at[f, hf, 0, 0], g.at[f, hf, 0, back], family, gather_sems.at[f, hf, k], along(1 - hf, OFFSETS[slot]))

    def gather2(f, hf, at, k):
        for slot, back in ((1, 2), (2, 1)):
            send(g.at[f, hf, 0, at], g.at[f, hf, back, at], 6, gather_sems.at[f, hf, k], along(hf, OFFSETS[slot]))

    def gather2_pass(f, hf, at, n, k):
        wait(g.at[f, hf, pl.ds(1, 2), at], gather_sems.at[f, hf, k])
        for back, way, q in ((2, 1, 0), (1, -1, 1)):
            rows_at = pl.ds(q * quarter, quarter)
            send(g.at[f, hf, back, at, rows_at], g.at[f, hf, 3, at, rows_at], 6,
                 gather_sems.at[f, hf, 5], along(hf, way))

    FIRST, NEAR, LAST = pl.ds(0, 1), pl.ds(1, 2), pl.ds(3, 1)

    def outer(f):
        norm_squared = jnp.sum(gathered(f, 1, n2, far), axis=(0, 1), keepdims=True)
        factor = jnp.minimum(1.0, CLIP_LEVEL * jnp.sqrt(F32(count)) / jnp.sqrt(norm_squared + 1e-06))
        for hf in both:
            at = pl.ds(hf * half_rows, half_rows)
            clipped = av[f, at] * factor
            moment = OUTER_MOMENTUM * mom[f, at] + clipped
            mout[f, at] = moment
            g[f, hf, 0, 0] = (clipped + OUTER_MOMENTUM * moment).astype(BF16)
            gather1(f, hf, 1, 5, 0)
            gather1(f, hf, 2, 5, 0)
            gather1(f, hf, 3, 5, 1)
        for hf in both:
            gather2(f, hf, FIRST, 2)

    def gather1_near(f, hf):
        wait(g.at[f, hf, 0, NEAR], gather_sems.at[f, hf, 0])
        gather2(f, hf, NEAR, 3)

    def gather1_far(f, hf):
        wait(g.at[f, hf, 0, LAST], gather_sems.at[f, hf, 1])
        gather2(f, hf, LAST, 4)
        hand_over(f, hf, 0, 1, 0)

    def gather2_first(f, hf):
        gather2_pass(f, hf, FIRST, 1, 2)

    def gather2_near(f, hf):
        gather2_pass(f, hf, NEAR, 2, 3)

    def gather2_far(f, hf):
        gather2_pass(f, hf, LAST, 1, 4)
        hand_over(f, hf, 1, 2, 1)

    def gather2_last(f, hf):
        wait(g.at[f, hf, 3], gather_sems.at[f, hf, 5])
        hand_over(f, hf, 3, 1, 2)

    def hand_over(f, hf, slot, n, k):
        at = pl.ds(slot, n)
        send(g.at[f, hf, at], h.at[f, hf, at], 7, hand_sems.at[f, hf, k], dev(0, 0, 1))

    def refresh(f, hf, slot, blocks, c):
        at = pl.ds(hf * half_rows, half_rows)

        @pl.loop(0, RING)
        def _(j):
            col = pl.ds(column(hf, OFFSETS[slot], offset(j), c), width)
            gw[f, at, col] = gw[f, at, col] - OUTER_RATE * blocks[f, hf, slot, j].astype(F32)

    def own(f, *slots):
        for hf in both:
            for slot in slots:
                refresh(f, hf, slot, g, core)

    def other(f, k):
        slot, n = ((0, 1), (1, 2), (3, 1))[k]
        for hf in both:
            wait(h.at[f, hf, pl.ds(slot, n)], hand_sems.at[f, hf, k])
            for i in range(n):
                refresh(f, hf, slot + i, h, 1 - core)

    steps = []

    def step(work, *args):
        steps.append((work, args))

    def halves(work, f):
        for hf in both:
            work(f, hf)

    def core_step(f, *slots):
        for slot in slots:
            for hf in both:
                if slot == 3:
                    load(f, hf)
                to_core(f, slot, hf)

    def far_step(f):
        from_core(f, 3)
        halves(ring1_far, f)

    def near_step(f):
        for slot in (1, 2):
            from_core(f, slot)
            for hf in both:
                ring1_near(f, hf, slot)

    step(core_step, 0, 3, 1, 2, 0)
    step(far_step, 0)
    step(near_step, 0)
    step(core_step, 1, 3, 1, 2, 0)
    step(halves, ring1_middle, 0)
    step(far_step, 1)
    step(near_step, 1)
    step(from_core, 0, 0)
    step(halves, ring2_open, 0)
    step(halves, ring1_middle, 1)
    step(norm_open, 0)
    step(from_core, 1, 0)
    step(halves, ring2_open, 1)
    step(norm_middle, 0)
    step(norm_open, 1)
    step(mom_load.wait)
    step(norm_middle, 1)
    step(outer, 0)
    step(halves, gather1_near, 0)
    step(halves, gather1_far, 0)
    step(outer, 1)
    step(halves, gather2_first, 0)
    step(halves, gather1_near, 1)
    step(halves, gather1_far, 1)
    step(halves, gather2_near, 0)
    step(halves, gather2_first, 1)
    step(halves, gather2_far, 0)
    step(own, 0, 0)
    step(other, 0, 0)
    step(halves, gather2_near, 1)
    step(own, 1, 0)
    step(halves, gather2_last, 0)
    step(halves, gather2_far, 1)
    step(other, 1, 0)
    step(own, 0, 1, 2)
    step(other, 0, 1)
    step(own, 0, 3)
    step(halves, gather2_last, 1)
    step(other, 0, 2)
    step(own, 1, 1, 2)
    step(other, 1, 1)
    step(own, 1, 3)
    step(other, 1, 2)
    for work, args in steps:
        work(*args)

    wait(ds, send_sems.at[0])
    wait(s_send, send_sems.at[1])
    wait(t_send, send_sems.at[2])
    wait(n1.at[:, pl.ds(0, len(near))], send_sems.at[3])
    wait(n2.at[:, pl.ds(0, len(far))], send_sems.at[4])
    wait(g.at[:, :, 0, pl.ds(0, 3)], send_sems.at[5])
    wait(g.at[:, :, pl.ds(0, 3)], send_sems.at[6])
    wait(h, send_sems.at[7])


def synchronize(local_weights, global_weights, momentum):
    frags, rows, cols = global_weights.shape
    width = momentum.shape[2]
    zs = lax.axis_size("fsdp")
    assert lax.axis_size("replica") == 2 * RING * RING and frags == 2
    half_rows, quarter = rows // 2, rows // 4
    anywhere = pl.BlockSpec(memory_space=pl.ANY)
    in_vmem = pl.BlockSpec(memory_space=pltpu.VMEM)
    dma = pltpu.SemaphoreType.DMA
    return pl.pallas_call(
        functools.partial(kernel, zs, rows * zs * cols),
        out_shape=(pltpu.VMEM(global_weights.shape, F32), pltpu.VMEM(momentum.shape, F32)),
        in_specs=[anywhere] * 3,
        out_specs=(in_vmem, in_vmem),
        scratch_shapes=[
            pltpu.VMEM((frags, rows, cols), BF16),
            pltpu.VMEM((frags, rows, width), F32),
            pltpu.VMEM((frags, RING, 2, RING, half_rows, width), BF16),
            pltpu.VMEM((frags, RING, 2, RING, half_rows, width), BF16),
            pltpu.VMEM((frags, 2, RING - 1, 2, RING, quarter, width), BF16),
            pltpu.VMEM((frags, 2, 2, RING, quarter, width), BF16),
            pltpu.VMEM((frags, 2, 2, 2, RING, quarter, width), BF16),
            pltpu.VMEM((frags, 2, half_rows, width), F32),
            pltpu.VMEM((frags, 2, RING - 1, half_rows, width), BF16),
            pltpu.VMEM((frags, 2, RING - 1, half_rows, width), BF16),
            pltpu.VMEM((frags, rows, width), F32),
            pltpu.VMEM((frags, 2 * zs, 8, 128), F32),
            pltpu.VMEM((frags, RING * RING, 8, 128), F32),
            pltpu.VMEM((frags, 2, RING, RING, half_rows, width), BF16),
            pltpu.VMEM((frags, 2, RING, RING, half_rows, width), BF16),
            dma((frags, 2, 3)),
            dma((8,)),
            dma((frags, 2)),
            dma((frags, RING)),
            dma((frags, 2)),
            dma((frags, 2)),
            dma((frags, 2)),
            dma((frags, 2, 6)),
            dma((frags, 2, 3)),
        ],
        compiler_params=pltpu.CompilerParams(
            collective_id=0, has_side_effects=True, vmem_limit_bytes=50 * 2**20
        ),
        cost_estimate=pl.CostEstimate(flops=20 * rows * cols, bytes_accessed=20 * frags * rows * cols // 2, transcendentals=0),
    )(local_weights, global_weights, momentum)


def solution(mesh):
    return jax.shard_map(
        synchronize,
        mesh=mesh,
        in_specs=(
            P("replica", None, "fsdp", None),
            P(None, "fsdp", None),
            P(None, "fsdp", "replica"),
        ),
        out_specs=(P(None, "fsdp", None), P(None, "fsdp", "replica")),
        check_vma=False,
    )
```

time: 484 us -> 58.1 us (0.12); the launches traced: 478 us -> 58 us
  other arithmetic: 140 us -> 0 us
  local copies, waits for them, and re-layouts: 136 us -> 4.1 us
  blocking collectives: 112 us -> 0 us
  Pallas kernels: 0 us -> 53.3 us
  waiting for transfers between devices: 41.4 us -> 0 us
  starting transfers between devices: 32.2 us -> 0 us
  between operations: 16 us -> 0.64 us
    unnamed x6 -> x0, other arithmetic: 92 us -> none
    convert_element_type x4 -> x0, local copies, waits for them, and re-layouts: 66.7 us -> none  [the longest x2 66.6 us: quantize(): (blocks / scales.astype(jnp.float32)[..., None]).astype(jnp.bfloat16)]
    psum x1 -> x0, blocking collectives: 65.8 us -> none  [synchronize(): norm_squared = lax.psum(squares, ('replica', 'fsdp'))]
    pallas_call x0 -> x1, Pallas kernels: none -> 53.3 us  [synchronize(): pl.pallas_call(functools.partial(kernel, zs, rows * zs * cols), out_shape...]
    unnamed x27 -> x2, local copies, waits for them, and re-layouts: 56 us -> 4.1 us
    all_gather x2 -> x0, blocking collectives: 46.2 us -> none  [synchronize(): lax.all_gather(step_scales, 'replica', axis=2, tiled=True)]
    all_gather x2 -> x0, waiting for transfers between devices: 32.9 us -> none  [synchronize(): lax.all_gather(step_codes, 'replica', axis=2, tiled=True)]
    all_to_all x4 -> x0, starting transfers between devices: 31.9 us -> none  [the longest x2 16.5 us: synchronize(): lax.all_to_all(block_scales[None], 'replica', split_axis=3, concat_axis=0...]
  transfers between devices with their start and end apart: 6 -> 0, of which waited for: 2 -> 0; matrix products, arithmetic and copies ran while one was open for 44% -> 0% of each run, Pallas kernels for 0% -> 0%
where the time goes in v2:
time: 58.1 us; the launch traced here: 58 us
  Pallas kernels  53.3 us (92%)
  local copies, waits for them, and re-layouts  4.1 us (7%)
  between operations  0.64 us (1%)
    pallas_call x1, Pallas kernels, synchronize(): pl.pallas_call(functools.partial(kernel, zs, rows * zs * cols), out_shape...  53.3 us
    unnamed x2, local copies, waits for them, and re-layouts  4.1 us

profile of v2, /device:TPU:1, one launch (start us, length us, event | category | flops | bytes accessed | tf_op | source)
XLA Modules:
  0.0 58.0 jit_solution(5238978420457079030)
XLA Ops:
  0.6 53.3 %shard_map.50 = (f32[2,128,8192]{2,1,0:T(8,128)S(1)}, f32[2,128,256]{2,1,0:T(8,128)S(1)}) custom-call(bf16[1,2,128,8192]{3,2,1,0:T(8,128)(2,1)} %lw_hbm.1, f32[2,128,8192]{2,1,0:T(8,128)} %gw_hbm.1, f32[2,128,256]{2,1,0:T(8,128)} %mom_hbm.1), custom_call_target="tpu_custom_call" | custom-call | flops 20971520 | bytes 20971520 | tf_op jit(solution)/shard_map/pallas_call | solution.py:343
  53.9 3.4 %copy.7 = f32[2,128,8192]{2,1,0:T(8,128)} copy(f32[2,128,8192]{2,1,0:T(8,128)S(1)} %get-tuple-element.2) | data formatting | bytes 16777216
  57.3 0.7 %copy.8 = f32[2,128,256]{2,1,0:T(8,128)} copy(f32[2,128,256]{2,1,0:T(8,128)S(1)} %get-tuple-element.3) | data formatting | bytes 524288

commit v3 on v2

--- a/solution.py
+++ b/solution.py
@@ -64,19 +64,19 @@
             for copy in loads[f, hf]:
                 copy.start()
 
+    mom_load = pltpu.make_async_copy(mom_hbm, mom, in_sems.at[0, 0, 2])
+    mom_load.start()
     start_loads(0)
 
     near = [(0, 0, oc, oz) for oz in range(zs) for oc in range(2) if (oc, oz) != (0, 0)]
     far = [(ox, oy, 0, 0) for ox in range(RING) for oy in range(RING) if (ox, oy) != (0, 0)]
-    greeted = near + [(1, 0, 0, 0), (-1, 0, 0, 0), (0, 1, 0, 0), (0, -1, 0, 0)]
+    greeted = near + [(o, 0, 0, 0) for o in OFFSETS[1:]] + [(0, o, 0, 0) for o in OFFSETS[1:]]
     barrier = pltpu.get_barrier_semaphore()
     for partner in greeted:
         pl.semaphore_signal(barrier, inc=1, device_id=dev(*partner), device_id_type=MESH)
     pl.semaphore_wait(barrier, len(greeted))
 
     start_loads(1)
-    mom_load = pltpu.make_async_copy(mom_hbm, mom, in_sems.at[0, 0, 2])
-    mom_load.start()
 
     def difference(f, row, n, col):
         at = pl.ds(row, n)
@@ -147,107 +147,137 @@
             part = part + t_end[f, hf, k].astype(F32)
         part = part * (1.0 / (2 * RING * RING))
         av[f, pl.ds(hf * half_rows, half_rows)] = part
+        return part
+
+    def tile(part):
         square = jnp.sum((part * part).reshape(half_rows // 8, 8, width), axis=0)
         total = square[:, :128]
         for c in range(1, width // 128):
             total = total + square[:, c * 128:(c + 1) * 128]
         return total
 
-    def exchange(f, stage, tiles, partners):
-        n = len(partners)
-        for i, partner in enumerate(partners):
-            send(tiles.at[f, n], tiles.at[f, i], 3 + stage, norm_sems.at[f, stage], dev(*partner))
+    def exchange(f, stage, tiles, me, partners):
+        for partner in partners:
+            send(tiles.at[f, me], tiles.at[f, me], 3 + stage, norm_sems.at[f, stage], dev(*partner))
 
     def gathered(f, stage, tiles, partners):
         wait(tiles.at[f, pl.ds(0, len(partners))], norm_sems.at[f, stage])
         return jnp.sum(tiles[f], axis=0)
 
     def norm_open(f):
-        n1[f, len(near)] = ring2_close(f, 0) + ring2_close(f, 1)
-        exchange(f, 0, n1, near)
+        at = pl.ds(half_rows, half_rows)
+        n1[f, z * 2 + core] = tile(av[f, pl.ds(0, half_rows)]) + tile(av[f, at])
+        exchange(f, 0, n1, z * 2 + core, near)
 
     def norm_middle(f):
-        n2[f, len(far)] = gathered(f, 0, n1, near)
-        exchange(f, 1, n2, far)
-
-    def gather1(f, hf, slot, family, k):
+        n2[f, x * RING + y] = gathered(f, 0, n1, near)
+        exchange(f, 1, n2, x * RING + y, far)
+
+    def factor_of(f):
+        norm_squared = jnp.sum(gathered(f, 1, n2, far), axis=(0, 1), keepdims=True)
+        return jnp.minimum(1.0, CLIP_LEVEL * jnp.sqrt(F32(count)) / jnp.sqrt(norm_squared + 1e-06))
+
+    STEP, AVERAGE, MOMENT = 0, 1, 2
+    FIRST, NEAR, LAST = pl.ds(0, 1), pl.ds(1, 2), pl.ds(3, 1)
+
+    def gather1(s, hf, slot, k):
         back = (None, 2, 1, 3)[slot]
-        send(g.at[f, hf, 0, 0], g.at[f, hf, 0, back], family, gather_sems.at[f, hf, k], along(1 - hf, OFFSETS[slot]))
-
-    def gather2(f, hf, at, k):
+        send(g.at[s, hf, 0, 0], g.at[s, hf, 0, back], 5, gather_sems.at[s, hf, k], along(1 - hf, OFFSETS[slot]))
+
+    def gather2(s, hf, at, k):
         for slot, back in ((1, 2), (2, 1)):
-            send(g.at[f, hf, 0, at], g.at[f, hf, back, at], 6, gather_sems.at[f, hf, k], along(hf, OFFSETS[slot]))
-
-    def gather2_pass(f, hf, at, n, k):
-        wait(g.at[f, hf, pl.ds(1, 2), at], gather_sems.at[f, hf, k])
+            send(g.at[s, hf, 0, at], g.at[s, hf, back, at], 6, gather_sems.at[s, hf, k], along(hf, OFFSETS[slot]))
+
+    def gather2_pass(s, hf, at, k):
+        wait(g.at[s, hf, pl.ds(1, 2), at], gather_sems.at[s, hf, k])
         for back, way, q in ((2, 1, 0), (1, -1, 1)):
             rows_at = pl.ds(q * quarter, quarter)
-            send(g.at[f, hf, back, at, rows_at], g.at[f, hf, 3, at, rows_at], 6,
-                 gather_sems.at[f, hf, 5], along(hf, way))
-
-    FIRST, NEAR, LAST = pl.ds(0, 1), pl.ds(1, 2), pl.ds(3, 1)
-
-    def outer(f):
-        norm_squared = jnp.sum(gathered(f, 1, n2, far), axis=(0, 1), keepdims=True)
-        factor = jnp.minimum(1.0, CLIP_LEVEL * jnp.sqrt(F32(count)) / jnp.sqrt(norm_squared + 1e-06))
+            send(g.at[s, hf, back, at, rows_at], g.at[s, hf, 3, at, rows_at], 6,
+                 gather_sems.at[s, hf, 5], along(hf, way))
+
+    def spread(s):
+        for hf in both:
+            for slot, k in ((1, 0), (2, 0), (3, 1)):
+                gather1(s, hf, slot, k)
+        for hf in both:
+            gather2(s, hf, FIRST, 2)
+
+    def spread_moment():
+        mom_load.wait()
+        for hf in both:
+            g[MOMENT, hf, 0, 0] = mom[1, pl.ds(hf * half_rows, half_rows)].astype(BF16)
+        spread(MOMENT)
+
+    def spread_average():
+        for hf in both:
+            g[AVERAGE, hf, 0, 0] = ring2_close(1, hf).astype(BF16)
+        spread(AVERAGE)
+
+    def spread_step():
+        factor = factor_of(0)
         for hf in both:
             at = pl.ds(hf * half_rows, half_rows)
-            clipped = av[f, at] * factor
-            moment = OUTER_MOMENTUM * mom[f, at] + clipped
-            mout[f, at] = moment
-            g[f, hf, 0, 0] = (clipped + OUTER_MOMENTUM * moment).astype(BF16)
-            gather1(f, hf, 1, 5, 0)
-            gather1(f, hf, 2, 5, 0)
-            gather1(f, hf, 3, 5, 1)
-        for hf in both:
-            gather2(f, hf, FIRST, 2)
-
-    def gather1_near(f, hf):
-        wait(g.at[f, hf, 0, NEAR], gather_sems.at[f, hf, 0])
-        gather2(f, hf, NEAR, 3)
-
-    def gather1_far(f, hf):
-        wait(g.at[f, hf, 0, LAST], gather_sems.at[f, hf, 1])
-        gather2(f, hf, LAST, 4)
-        hand_over(f, hf, 0, 1, 0)
-
-    def gather2_first(f, hf):
-        gather2_pass(f, hf, FIRST, 1, 2)
-
-    def gather2_near(f, hf):
-        gather2_pass(f, hf, NEAR, 2, 3)
-
-    def gather2_far(f, hf):
-        gather2_pass(f, hf, LAST, 1, 4)
-        hand_over(f, hf, 1, 2, 1)
-
-    def gather2_last(f, hf):
-        wait(g.at[f, hf, 3], gather_sems.at[f, hf, 5])
-        hand_over(f, hf, 3, 1, 2)
-
-    def hand_over(f, hf, slot, n, k):
+            clipped = av[0, at] * factor
+            moment = OUTER_MOMENTUM * mom[0, at] + clipped
+            mout[0, at] = moment
+            g[STEP, hf, 0, 0] = (clipped + OUTER_MOMENTUM * moment).astype(BF16)
+        spread(STEP)
+
+    scales = {STEP: OUTER_RATE, MOMENT: OUTER_RATE * OUTER_MOMENTUM * OUTER_MOMENTUM}
+
+    def clip_average():
+        factor = factor_of(1)
+        mout[1] = OUTER_MOMENTUM * mom[1] + av[1] * factor
+        scales[AVERAGE] = OUTER_RATE * (1.0 + OUTER_MOMENTUM) * factor
+
+    def gather1_near(s, hf):
+        wait(g.at[s, hf, 0, NEAR], gather_sems.at[s, hf, 0])
+        gather2(s, hf, NEAR, 3)
+
+    def gather1_far(s, hf):
+        wait(g.at[s, hf, 0, LAST], gather_sems.at[s, hf, 1])
+        gather2(s, hf, LAST, 4)
+        hand_over(s, hf, 0, 1, 0)
+
+    def gather2_first(s, hf):
+        gather2_pass(s, hf, FIRST, 2)
+
+    def gather2_near(s, hf):
+        gather2_pass(s, hf, NEAR, 3)
+
+    def gather2_far(s, hf):
+        gather2_pass(s, hf, LAST, 4)
+        hand_over(s, hf, 1, 2, 1)
+
+    def gather2_last(s, hf):
+        wait(g.at[s, hf, 3], gather_sems.at[s, hf, 5])
+        hand_over(s, hf, 3, 1, 2)
+
+    def hand_over(s, hf, slot, n, k):
         at = pl.ds(slot, n)
-        send(g.at[f, hf, at], h.at[f, hf, at], 7, hand_sems.at[f, hf, k], dev(0, 0, 1))
-
-    def refresh(f, hf, slot, blocks, c):
+        send(g.at[s, hf, at], h.at[s, hf, at], 7, hand_sems.at[s, hf, k], dev(0, 0, 1))
+
+    def refresh(s, hf, slot, blocks, c):
+        f = 0 if s == STEP else 1
         at = pl.ds(hf * half_rows, half_rows)
+        scale = scales[s]
 
         @pl.loop(0, RING)
         def _(j):
             col = pl.ds(column(hf, OFFSETS[slot], offset(j), c), width)
-            gw[f, at, col] = gw[f, at, col] - OUTER_RATE * blocks[f, hf, slot, j].astype(F32)
-
-    def own(f, *slots):
+            gw[f, at, col] = gw[f, at, col] - scale * blocks[s, hf, slot, j].astype(F32)
+
+    def own(s, *slots):
         for hf in both:
             for slot in slots:
-                refresh(f, hf, slot, g, core)
-
-    def other(f, k):
+                refresh(s, hf, slot, g, core)
+
+    def other(s, k):
         slot, n = ((0, 1), (1, 2), (3, 1))[k]
         for hf in both:
-            wait(h.at[f, hf, pl.ds(slot, n)], hand_sems.at[f, hf, k])
+            wait(h.at[s, hf, pl.ds(slot, n)], hand_sems.at[s, hf, k])
             for i in range(n):
-                refresh(f, hf, slot + i, h, 1 - core)
+                refresh(s, hf, slot + i, h, 1 - core)
 
     steps = []
 
@@ -258,66 +288,91 @@
         for hf in both:
             work(f, hf)
 
-    def core_step(f, *slots):
-        for slot in slots:
-            for hf in both:
-                if slot == 3:
-                    load(f, hf)
-                to_core(f, slot, hf)
+    def core_step(f, slot):
+        for hf in both:
+            if slot == 3:
+                load(f, hf)
+            to_core(f, slot, hf)
 
     def far_step(f):
         from_core(f, 3)
         halves(ring1_far, f)
 
-    def near_step(f):
-        for slot in (1, 2):
-            from_core(f, slot)
-            for hf in both:
-                ring1_near(f, hf, slot)
-
-    step(core_step, 0, 3, 1, 2, 0)
+    def near_step(f, slot):
+        from_core(f, slot)
+        for hf in both:
+            ring1_near(f, hf, slot)
+
+    def open_step(f):
+        from_core(f, 0)
+        halves(ring2_open, f)
+
+    def close_step(f):
+        for hf in both:
+            ring2_close(f, hf)
+
+    step(core_step, 0, 3)
+    step(core_step, 0, 1)
+    step(spread_moment)
     step(far_step, 0)
-    step(near_step, 0)
-    step(core_step, 1, 3, 1, 2, 0)
+    step(core_step, 0, 2)
+    step(near_step, 0, 1)
+    step(core_step, 0, 0)
+    step(near_step, 0, 2)
+    step(core_step, 1, 3)
+    step(core_step, 1, 1)
+    step(core_step, 1, 2)
+    step(far_step, 1)
+    step(core_step, 1, 0)
     step(halves, ring1_middle, 0)
-    step(far_step, 1)
-    step(near_step, 1)
-    step(from_core, 0, 0)
-    step(halves, ring2_open, 0)
+    step(near_step, 1, 1)
+    step(near_step, 1, 2)
     step(halves, ring1_middle, 1)
+    step(open_step, 0)
+    step(halves, gather1_near, MOMENT)
+    step(open_step, 1)
+    step(halves, gather1_far, MOMENT)
+    step(halves, gather2_first, MOMENT)
+    step(close_step, 0)
     step(norm_open, 0)
-    step(from_core, 1, 0)
-    step(halves, ring2_open, 1)
+    step(halves, gather2_near, MOMENT)
+    step(spread_average)
+    step(norm_open, 1)
     step(norm_middle, 0)
-    step(norm_open, 1)
-    step(mom_load.wait)
+    step(halves, gather2_far, MOMENT)
+    step(own, MOMENT, 0)
+    step(halves, gather1_near, AVERAGE)
+    step(halves, gather1_far, AVERAGE)
     step(norm_middle, 1)
-    step(outer, 0)
-    step(halves, gather1_near, 0)
-    step(halves, gather1_far, 0)
-    step(outer, 1)
-    step(halves, gather2_first, 0)
-    step(halves, gather1_near, 1)
-    step(halves, gather1_far, 1)
-    step(halves, gather2_near, 0)
-    step(halves, gather2_first, 1)
-    step(halves, gather2_far, 0)
-    step(own, 0, 0)
-    step(other, 0, 0)
-    step(halves, gather2_near, 1)
-    step(own, 1, 0)
-    step(halves, gather2_last, 0)
-    step(halves, gather2_far, 1)
-    step(other, 1, 0)
-    step(own, 0, 1, 2)
-    step(other, 0, 1)
-    step(own, 0, 3)
-    step(halves, gather2_last, 1)
-    step(other, 0, 2)
-    step(own, 1, 1, 2)
-    step(other, 1, 1)
-    step(own, 1, 3)
-    step(other, 1, 2)
+    step(spread_step)
+    step(halves, gather2_first, AVERAGE)
+    step(halves, gather2_last, MOMENT)
+    step(other, MOMENT, 0)
+    step(halves, gather2_near, AVERAGE)
+    step(halves, gather1_near, STEP)
+    step(halves, gather1_far, STEP)
+    step(halves, gather2_far, AVERAGE)
+    step(halves, gather2_first, STEP)
+    step(clip_average)
+    step(own, MOMENT, 1, 2, 3)
+    step(other, MOMENT, 1)
+    step(halves, gather2_near, STEP)
+    step(other, MOMENT, 2)
+    step(own, AVERAGE, 0)
+    step(other, AVERAGE, 0)
+    step(halves, gather2_last, AVERAGE)
+    step(halves, gather2_far, STEP)
+    step(own, AVERAGE, 1, 2)
+    step(other, AVERAGE, 1)
+    step(own, STEP, 0)
+    step(other, STEP, 0)
+    step(own, AVERAGE, 3)
+    step(other, AVERAGE, 2)
+    step(halves, gather2_last, STEP)
+    step(own, STEP, 1, 2)
+    step(other, STEP, 1)
+    step(own, STEP, 3)
+    step(other, STEP, 2)
     for work, args in steps:
         work(*args)
 
@@ -359,8 +414,8 @@
             pltpu.VMEM((frags, rows, width), F32),
             pltpu.VMEM((frags, 2 * zs, 8, 128), F32),
             pltpu.VMEM((frags, RING * RING, 8, 128), F32),
-            pltpu.VMEM((frags, 2, RING, RING, half_rows, width), BF16),
-            pltpu.VMEM((frags, 2, RING, RING, half_rows, width), BF16),
+            pltpu.VMEM((frags + 1, 2, RING, RING, half_rows, width), BF16),
+            pltpu.VMEM((frags + 1, 2, RING, RING, half_rows, width), BF16),
             dma((frags, 2, 3)),
             dma((8,)),
             dma((frags, 2)),
@@ -368,8 +423,8 @@
             dma((frags, 2)),
             dma((frags, 2)),
             dma((frags, 2)),
-            dma((frags, 2, 6)),
-            dma((frags, 2, 3)),
+            dma((frags + 1, 2, 6)),
+            dma((frags + 1, 2, 3)),
         ],
         compiler_params=pltpu.CompilerParams(
             collective_id=0, has_side_effects=True, vmem_limit_bytes=50 * 2**20

time: 58.1 us -> 52.6 us (0.905)
  Pallas kernels: 53.3 us -> 47.8 us
    pallas_call x1, Pallas kernels: 53.3 us -> 47.8 us  [synchronize(): pl.pallas_call(functools.partial(kernel, zs, rows * zs * cols), out_shape...]
where the time goes in v3:
time: 52.6 us; the launch traced here: 52.5 us
  Pallas kernels  47.8 us (91%)
  local copies, waits for them, and re-layouts  4.1 us (8%)
  between operations  0.64 us (1%)
    pallas_call x1, Pallas kernels, synchronize(): pl.pallas_call(functools.partial(kernel, zs, rows * zs * cols), out_shape...  47.8 us
    unnamed x2, local copies, waits for them, and re-layouts  4.1 us

profile of v3, /device:TPU:1, one launch (start us, length us, event | category | flops | bytes accessed | tf_op | source)
XLA Modules:
  0.0 52.5 jit_solution(5684644720809905668)
XLA Ops:
  0.6 47.8 %shard_map.50 = (f32[2,128,8192]{2,1,0:T(8,128)S(1)}, f32[2,128,256]{2,1,0:T(8,128)S(1)}) custom-call(bf16[1,2,128,8192]{3,2,1,0:T(8,128)(2,1)} %lw_hbm.1, f32[2,128,8192]{2,1,0:T(8,128)} %gw_hbm.1, f32[2,128,256]{2,1,0:T(8,128)} %mom_hbm.1), custom_call_target="tpu_custom_call" | custom-call | flops 20971520 | bytes 20971520 | tf_op jit(solution)/shard_map/pallas_call | solution.py:398
  48.4 3.4 %copy.7 = f32[2,128,8192]{2,1,0:T(8,128)} copy(f32[2,128,8192]{2,1,0:T(8,128)S(1)} %get-tuple-element.2) | data formatting | bytes 16777216
  51.8 0.7 %copy.8 = f32[2,128,256]{2,1,0:T(8,128)} copy(f32[2,128,256]{2,1,0:T(8,128)S(1)} %get-tuple-element.3) | data formatting | bytes 524288

commit v4 on v3

--- a/solution.py
+++ b/solution.py
@@ -18,7 +18,7 @@
 
 def kernel(zs, count, lw_hbm, gw_hbm, mom_hbm, gw, mout,
            lw, mom, ds, dr, s_send, s_mid, s_end, tt, t_send, t_end, av, n1, n2, g, h,
-           in_sems, send_sems, norm_sems, core_sems, mid_sems, end_sems, end2_sems, gather_sems, hand_sems):
+           in_sems, mom_sem, send_sems, norm_sems, core_sems, mid_sems, end_sems, end2_sems, gather_sems, hand_sems):
     frags, rows, _ = gw.shape
     width = mom.shape[2]
     half_rows, quarter = rows // 2, rows // 4
@@ -64,7 +64,7 @@
             for copy in loads[f, hf]:
                 copy.start()
 
-    mom_load = pltpu.make_async_copy(mom_hbm, mom, in_sems.at[0, 0, 2])
+    mom_load = pltpu.make_async_copy(mom_hbm, mom, mom_sem)
     mom_load.start()
     start_loads(0)
 
@@ -106,7 +106,7 @@
             @pl.loop(0, RING)
             def _(j):
                 s_send[f, hf, 2, q, j] = pair_sum(f, hf, 3, j, q * quarter, quarter).astype(BF16)
-            send(s_send.at[f, hf, 2, q], s_mid.at[f, hf, q], 1, mid_sems.at[f, hf], along(hf, way))
+            send(s_send.at[f, hf, 2, q], s_mid.at[f, hf, q], 1, mid_sems.at[f], along(hf, way))
 
     def ring1_near(f, hf, slot):
         q, way = (1, 1) if slot == 1 else (0, -1)
@@ -114,20 +114,17 @@
         @pl.loop(0, RING)
         def _(j):
             s_send[f, hf, slot - 1, q, j] = pair_sum(f, hf, slot, j, q * quarter, quarter).astype(BF16)
-        send(s_send.at[f, hf, slot - 1, q], s_end.at[f, hf, slot - 1, q], 1, end_sems.at[f, hf], along(hf, way))
+        send(s_send.at[f, hf, slot - 1, q], s_end.at[f, hf, slot - 1, q], 1, end_sems.at[f], along(hf, way))
 
     def ring1_middle(f, hf):
-        wait(s_mid.at[f, hf], mid_sems.at[f, hf])
         for slot, q, way in ((1, 0, 1), (2, 1, -1)):
             @pl.loop(0, RING)
             def _(j):
                 total = pair_sum(f, hf, slot, j, q * quarter, quarter) + s_mid[f, hf, q, j].astype(F32)
                 s_send[f, hf, slot - 1, q, j] = total.astype(BF16)
-            send(s_send.at[f, hf, slot - 1, q], s_end.at[f, hf, slot - 1, q], 1, end_sems.at[f, hf], along(hf, way))
+            send(s_send.at[f, hf, slot - 1, q], s_end.at[f, hf, slot - 1, q], 1, end_sems.at[f], along(hf, way))
 
     def ring2_open(f, hf):
-        wait(s_end.at[f, hf], end_sems.at[f, hf])
-
         def whole(j, q):
             total = pair_sum(f, hf, 0, j, q * quarter, quarter)
             return total + s_end[f, hf, 0, q, j].astype(F32) + s_end[f, hf, 1, q, j].astype(F32)
@@ -135,13 +132,12 @@
         for slot in (3, 1, 2):
             for q in both:
                 t_send[f, hf, slot - 1, pl.ds(q * quarter, quarter)] = whole(slot, q).astype(BF16)
-            send(t_send.at[f, hf, slot - 1], t_end.at[f, hf, slot - 1], 2, end2_sems.at[f, hf],
+            send(t_send.at[f, hf, slot - 1], t_end.at[f, hf, slot - 1], 2, end2_sems.at[f],
                  along(1 - hf, OFFSETS[slot]))
         for q in both:
             tt[f, hf, pl.ds(q * quarter, quarter)] = whole(0, q)
 
     def ring2_close(f, hf):
-        wait(t_end.at[f, hf], end2_sems.at[f, hf])
         part = tt[f, hf]
         for k in range(RING - 1):
             part = part + t_end[f, hf, k].astype(F32)
@@ -182,18 +178,17 @@
 
     def gather1(s, hf, slot, k):
         back = (None, 2, 1, 3)[slot]
-        send(g.at[s, hf, 0, 0], g.at[s, hf, 0, back], 5, gather_sems.at[s, hf, k], along(1 - hf, OFFSETS[slot]))
+        send(g.at[s, hf, 0, 0], g.at[s, hf, 0, back], 5, gather_sems.at[s, k], along(1 - hf, OFFSETS[slot]))
 
     def gather2(s, hf, at, k):
         for slot, back in ((1, 2), (2, 1)):
-            send(g.at[s, hf, 0, at], g.at[s, hf, back, at], 6, gather_sems.at[s, hf, k], along(hf, OFFSETS[slot]))
+            send(g.at[s, hf, 0, at], g.at[s, hf, back, at], 6, gather_sems.at[s, k], along(hf, OFFSETS[slot]))
 
     def gather2_pass(s, hf, at, k):
-        wait(g.at[s, hf, pl.ds(1, 2), at], gather_sems.at[s, hf, k])
         for back, way, q in ((2, 1, 0), (1, -1, 1)):
             rows_at = pl.ds(q * quarter, quarter)
             send(g.at[s, hf, back, at, rows_at], g.at[s, hf, 3, at, rows_at], 6,
-                 gather_sems.at[s, hf, 5], along(hf, way))
+                 gather_sems.at[s, 5], along(hf, way))
 
     def spread(s):
         for hf in both:
@@ -209,6 +204,7 @@
         spread(MOMENT)
 
     def spread_average():
+        wait(t_end.at[1], end2_sems.at[1])
         for hf in both:
             g[AVERAGE, hf, 0, 0] = ring2_close(1, hf).astype(BF16)
         spread(AVERAGE)
@@ -230,32 +226,42 @@
         mout[1] = OUTER_MOMENTUM * mom[1] + av[1] * factor
         scales[AVERAGE] = OUTER_RATE * (1.0 + OUTER_MOMENTUM) * factor
 
-    def gather1_near(s, hf):
-        wait(g.at[s, hf, 0, NEAR], gather_sems.at[s, hf, 0])
-        gather2(s, hf, NEAR, 3)
-
-    def gather1_far(s, hf):
-        wait(g.at[s, hf, 0, LAST], gather_sems.at[s, hf, 1])
-        gather2(s, hf, LAST, 4)
-        hand_over(s, hf, 0, 1, 0)
-
-    def gather2_first(s, hf):
-        gather2_pass(s, hf, FIRST, 2)
-
-    def gather2_near(s, hf):
-        gather2_pass(s, hf, NEAR, 3)
-
-    def gather2_far(s, hf):
-        gather2_pass(s, hf, LAST, 4)
-        hand_over(s, hf, 1, 2, 1)
-
-    def gather2_last(s, hf):
-        wait(g.at[s, hf, 3], gather_sems.at[s, hf, 5])
-        hand_over(s, hf, 3, 1, 2)
+    def gather1_near(s):
+        wait(g.at[s, :, 0, NEAR], gather_sems.at[s, 0])
+        for hf in both:
+            gather2(s, hf, NEAR, 3)
+
+    def gather1_far(s):
+        wait(g.at[s, :, 0, LAST], gather_sems.at[s, 1])
+        for hf in both:
+            gather2(s, hf, LAST, 4)
+        for hf in both:
+            hand_over(s, hf, 0, 1, 0)
+
+    def gather2_passes(s, at, k):
+        wait(g.at[s, :, pl.ds(1, 2), at], gather_sems.at[s, k])
+        for hf in both:
+            gather2_pass(s, hf, at, k)
+
+    def gather2_first(s):
+        gather2_passes(s, FIRST, 2)
+
+    def gather2_near(s):
+        gather2_passes(s, NEAR, 3)
+
+    def gather2_far(s):
+        gather2_passes(s, LAST, 4)
+        for hf in both:
+            hand_over(s, hf, 1, 2, 1)
+
+    def gather2_last(s):
+        wait(g.at[s, :, 3], gather_sems.at[s, 5])
+        for hf in both:
+            hand_over(s, hf, 3, 1, 2)
 
     def hand_over(s, hf, slot, n, k):
         at = pl.ds(slot, n)
-        send(g.at[s, hf, at], h.at[s, hf, at], 7, hand_sems.at[s, hf, k], dev(0, 0, 1))
+        send(g.at[s, hf, at], h.at[s, hf, at], 7, hand_sems.at[s, k], dev(0, 0, 1))
 
     def refresh(s, hf, slot, blocks, c):
         f = 0 if s == STEP else 1
@@ -274,8 +280,8 @@
 
     def other(s, k):
         slot, n = ((0, 1), (1, 2), (3, 1))[k]
-        for hf in both:
-            wait(h.at[s, hf, pl.ds(slot, n)], hand_sems.at[s, hf, k])
+        wait(h.at[s, :, pl.ds(slot, n)], hand_sems.at[s, k])
+        for hf in both:
             for i in range(n):
                 refresh(s, hf, slot + i, h, 1 - core)
 
@@ -303,17 +309,22 @@
         for hf in both:
             ring1_near(f, hf, slot)
 
+    def middle_step(f):
+        wait(s_mid.at[f], mid_sems.at[f])
+        halves(ring1_middle, f)
+
     def open_step(f):
         from_core(f, 0)
+        wait(s_end.at[f], end_sems.at[f])
         halves(ring2_open, f)
 
     def close_step(f):
-        for hf in both:
-            ring2_close(f, hf)
-
+        wait(t_end.at[f], end2_sems.at[f])
+        halves(ring2_close, f)
+
+    step(spread_moment)
     step(core_step, 0, 3)
     step(core_step, 0, 1)
-    step(spread_moment)
     step(far_step, 0)
     step(core_step, 0, 2)
     step(near_step, 0, 1)
@@ -324,51 +335,51 @@
     step(core_step, 1, 2)
     step(far_step, 1)
     step(core_step, 1, 0)
-    step(halves, ring1_middle, 0)
+    step(middle_step, 0)
     step(near_step, 1, 1)
     step(near_step, 1, 2)
-    step(halves, ring1_middle, 1)
+    step(middle_step, 1)
     step(open_step, 0)
-    step(halves, gather1_near, MOMENT)
+    step(gather1_near, MOMENT)
     step(open_step, 1)
-    step(halves, gather1_far, MOMENT)
-    step(halves, gather2_first, MOMENT)
     step(close_step, 0)
     step(norm_open, 0)
-    step(halves, gather2_near, MOMENT)
+    step(gather1_far, MOMENT)
+    step(gather2_first, MOMENT)
+    step(gather2_near, MOMENT)
     step(spread_average)
+    step(norm_middle, 0)
     step(norm_open, 1)
-    step(norm_middle, 0)
-    step(halves, gather2_far, MOMENT)
+    step(gather2_far, MOMENT)
     step(own, MOMENT, 0)
-    step(halves, gather1_near, AVERAGE)
-    step(halves, gather1_far, AVERAGE)
+    step(gather1_near, AVERAGE)
     step(norm_middle, 1)
+    step(gather1_far, AVERAGE)
+    step(gather2_first, AVERAGE)
     step(spread_step)
-    step(halves, gather2_first, AVERAGE)
-    step(halves, gather2_last, MOMENT)
+    step(gather2_last, MOMENT)
     step(other, MOMENT, 0)
-    step(halves, gather2_near, AVERAGE)
-    step(halves, gather1_near, STEP)
-    step(halves, gather1_far, STEP)
-    step(halves, gather2_far, AVERAGE)
-    step(halves, gather2_first, STEP)
+    step(gather2_near, AVERAGE)
+    step(gather2_far, AVERAGE)
+    step(gather1_near, STEP)
+    step(gather1_far, STEP)
+    step(own, MOMENT, 1)
+    step(gather2_first, STEP)
     step(clip_average)
-    step(own, MOMENT, 1, 2, 3)
+    step(own, MOMENT, 2, 3)
     step(other, MOMENT, 1)
-    step(halves, gather2_near, STEP)
+    step(gather2_last, AVERAGE)
+    step(gather2_near, STEP)
+    step(gather2_far, STEP)
     step(other, MOMENT, 2)
-    step(own, AVERAGE, 0)
+    step(own, AVERAGE, 0, 1, 2)
     step(other, AVERAGE, 0)
-    step(halves, gather2_last, AVERAGE)
-    step(halves, gather2_far, STEP)
-    step(own, AVERAGE, 1, 2)
+    step(own, STEP, 0)
+    step(gather2_last, STEP)
+    step(other, STEP, 0)
     step(other, AVERAGE, 1)
-    step(own, STEP, 0)
-    step(other, STEP, 0)
     step(own, AVERAGE, 3)
     step(other, AVERAGE, 2)
-    step(halves, gather2_last, STEP)
     step(own, STEP, 1, 2)
     step(other, STEP, 1)
     step(own, STEP, 3)
@@ -416,15 +427,16 @@
             pltpu.VMEM((frags, RING * RING, 8, 128), F32),
             pltpu.VMEM((frags + 1, 2, RING, RING, half_rows, width), BF16),
             pltpu.VMEM((frags + 1, 2, RING, RING, half_rows, width), BF16),
-            dma((frags, 2, 3)),
+            dma((frags, 2, 2)),
+            dma,
             dma((8,)),
             dma((frags, 2)),
             dma((frags, RING)),
-            dma((frags, 2)),
-            dma((frags, 2)),
-            dma((frags, 2)),
-            dma((frags + 1, 2, 6)),
-            dma((frags + 1, 2, 3)),
+            dma((frags,)),
+            dma((frags,)),
+            dma((frags,)),
+            dma((frags + 1, 6)),
+            dma((frags + 1, 3)),
         ],
         compiler_params=pltpu.CompilerParams(
             collective_id=0, has_side_effects=True, vmem_limit_bytes=50 * 2**20

time: 52.6 us -> 52.2 us (level)
  no operation moved by 1% of the time
where the time goes in v4:
time: 52.2 us; the launch traced here: 52 us
  Pallas kernels  47.3 us (91%)
  local copies, waits for them, and re-layouts  4.1 us (8%)
  between operations  0.64 us (1%)
    pallas_call x1, Pallas kernels, synchronize(): pl.pallas_call(functools.partial(kernel, zs, rows * zs * cols), out_shape...  47.3 us
    unnamed x2, local copies, waits for them, and re-layouts  4.1 us

profile of v4, /device:TPU:1, one launch (start us, length us, event | category | flops | bytes accessed | tf_op | source)
XLA Modules:
  0.0 52.0 jit_solution(8101993893077339148)
XLA Ops:
  0.6 47.3 %shard_map.50 = (f32[2,128,8192]{2,1,0:T(8,128)S(1)}, f32[2,128,256]{2,1,0:T(8,128)S(1)}) custom-call(bf16[1,2,128,8192]{3,2,1,0:T(8,128)(2,1)} %lw_hbm.1, f32[2,128,8192]{2,1,0:T(8,128)} %gw_hbm.1, f32[2,128,256]{2,1,0:T(8,128)} %mom_hbm.1), custom_call_target="tpu_custom_call" | custom-call | flops 20971520 | bytes 20971520 | tf_op jit(solution)/shard_map/pallas_call | solution.py:409
  47.9 3.4 %copy.7 = f32[2,128,8192]{2,1,0:T(8,128)} copy(f32[2,128,8192]{2,1,0:T(8,128)S(1)} %get-tuple-element.2) | data formatting | bytes 16777216
  51.3 0.7 %copy.8 = f32[2,128,256]{2,1,0:T(8,128)} copy(f32[2,128,256]{2,1,0:T(8,128)S(1)} %get-tuple-element.3) | data formatting | bytes 524288

commit v5 on v4

--- a/solution.py
+++ b/solution.py
@@ -18,7 +18,7 @@
 
 def kernel(zs, count, lw_hbm, gw_hbm, mom_hbm, gw, mout,
            lw, mom, ds, dr, s_send, s_mid, s_end, tt, t_send, t_end, av, n1, n2, g, h,
-           in_sems, mom_sem, send_sems, norm_sems, core_sems, mid_sems, end_sems, end2_sems, gather_sems, hand_sems):
+           in_sems, mom_sem, late_sem, send_sems, norm_sems, core_sems, mid_sems, end_sems, end2_sems, gather_sems, hand_sems):
     frags, rows, _ = gw.shape
     width = mom.shape[2]
     half_rows, quarter = rows // 2, rows // 4
@@ -51,40 +51,58 @@
     def wait(ref, sem):
         pltpu.make_async_copy(ref, ref, sem).wait()
 
-    loads = {}
-    for f in range(frags):
+    mom_load = pltpu.make_async_copy(mom_hbm, mom, mom_sem)
+    group = RING * 2 * width
+
+    def start_load(slot):
         for hf in both:
             at = pl.ds(hf * half_rows, half_rows)
-            loads[f, hf] = [
-                pltpu.make_async_copy(gw_hbm.at[f, at], gw.at[f, at], in_sems.at[f, hf, 0]),
-                pltpu.make_async_copy(lw_hbm.at[0, f, at], lw.at[f, at], in_sems.at[f, hf, 1])]
-
-    def start_loads(f):
-        for hf in both:
-            for copy in loads[f, hf]:
-                copy.start()
-
-    mom_load = pltpu.make_async_copy(mom_hbm, mom, mom_sem)
+            a = (x if hf == 0 else y) + OFFSETS[slot] + RING
+            if hf == 0:
+                columns = [pl.ds(pl.multiple_of(a % RING * group, group), group)]
+            else:
+                n = 2 * width
+                columns = [pl.ds(pl.multiple_of((b * RING + a % RING) * n, n), n) for b in range(RING)]
+            for col in columns:
+                pltpu.make_async_copy(gw_hbm.at[0, at, col], gw.at[0, at, col], in_sems.at[slot, 0]).start()
+                pltpu.make_async_copy(lw_hbm.at[0, 0, at, col], lw.at[0, at, col], in_sems.at[slot, 1]).start()
+
+    later = [
+        (pltpu.make_async_copy(gw_hbm.at[1], gw.at[1], in_sems.at[RING, 0])),
+        (pltpu.make_async_copy(lw_hbm.at[0, 1], lw.at[1], in_sems.at[RING, 1]))]
+
+    def load(f, slot):
+        if f == 0:
+            wait(gw.at[0, :, pl.ds(0, group)], in_sems.at[slot, 0])
+            wait(lw.at[0, :, pl.ds(0, group)], in_sems.at[slot, 1])
+        elif slot == 3:
+            for copy in later:
+                copy.wait()
+
+    start_load(3)
     mom_load.start()
-    start_loads(0)
 
     near = [(0, 0, oc, oz) for oz in range(zs) for oc in range(2) if (oc, oz) != (0, 0)]
     far = [(ox, oy, 0, 0) for ox in range(RING) for oy in range(RING) if (ox, oy) != (0, 0)]
-    greeted = near + [(o, 0, 0, 0) for o in OFFSETS[1:]] + [(0, o, 0, 0) for o in OFFSETS[1:]]
+    greeted = [(0, 0, 1, 0)] + [p for o in (1, -1) for p in ((o, 0, 0, 0), (0, o, 0, 0), (0, 0, 0, o))]
     barrier = pltpu.get_barrier_semaphore()
     for partner in greeted:
         pl.semaphore_signal(barrier, inc=1, device_id=dev(*partner), device_id_type=MESH)
+    for slot in (1, 2, 0):
+        start_load(slot)
     pl.semaphore_wait(barrier, len(greeted))
 
-    start_loads(1)
+    for o in (1, -1):
+        pl.semaphore_signal(late_sem, inc=1, device_id=dev(0, 0, 0, o), device_id_type=MESH)
+    for copy in later:
+        copy.start()
+
+    def known():
+        pl.semaphore_wait(late_sem, 2)
 
     def difference(f, row, n, col):
         at = pl.ds(row, n)
         return gw[f, at, pl.ds(col, width)] - lw[f, at, pl.ds(col, width)].astype(F32)
-
-    def load(f, hf):
-        for copy in loads[f, hf]:
-            copy.wait()
 
     def to_core(f, slot, hf):
         @pl.loop(0, RING)
@@ -143,7 +161,6 @@
             part = part + t_end[f, hf, k].astype(F32)
         part = part * (1.0 / (2 * RING * RING))
         av[f, pl.ds(hf * half_rows, half_rows)] = part
-        return part
 
     def tile(part):
         square = jnp.sum((part * part).reshape(half_rows // 8, 8, width), axis=0)
@@ -162,15 +179,15 @@
 
     def norm_open(f):
         at = pl.ds(half_rows, half_rows)
-        n1[f, z * 2 + core] = tile(av[f, pl.ds(0, half_rows)]) + tile(av[f, at])
+        n2[f, x * RING + y] = tile(av[f, pl.ds(0, half_rows)]) + tile(av[f, at])
+        exchange(f, 1, n2, x * RING + y, far)
+
+    def norm_middle(f):
+        n1[f, z * 2 + core] = gathered(f, 1, n2, far)
         exchange(f, 0, n1, z * 2 + core, near)
 
-    def norm_middle(f):
-        n2[f, x * RING + y] = gathered(f, 0, n1, near)
-        exchange(f, 1, n2, x * RING + y, far)
-
     def factor_of(f):
-        norm_squared = jnp.sum(gathered(f, 1, n2, far), axis=(0, 1), keepdims=True)
+        norm_squared = jnp.sum(gathered(f, 0, n1, near), axis=(0, 1), keepdims=True)
         return jnp.minimum(1.0, CLIP_LEVEL * jnp.sqrt(F32(count)) / jnp.sqrt(norm_squared + 1e-06))
 
     STEP, AVERAGE, MOMENT = 0, 1, 2
@@ -185,15 +202,16 @@
             send(g.at[s, hf, 0, at], g.at[s, hf, back, at], 6, gather_sems.at[s, k], along(hf, OFFSETS[slot]))
 
     def gather2_pass(s, hf, at, k):
+        k = 6 if k == 4 else 5
         for back, way, q in ((2, 1, 0), (1, -1, 1)):
             rows_at = pl.ds(q * quarter, quarter)
             send(g.at[s, hf, back, at, rows_at], g.at[s, hf, 3, at, rows_at], 6,
-                 gather_sems.at[s, 5], along(hf, way))
+                 gather_sems.at[s, k], along(hf, way))
 
     def spread(s):
         for hf in both:
-            for slot, k in ((1, 0), (2, 0), (3, 1)):
-                gather1(s, hf, slot, k)
+            for slot in (1, 2, 3)[:2 if s == MOMENT else 3]:
+                gather1(s, hf, slot, slot // 3)
         for hf in both:
             gather2(s, hf, FIRST, 2)
 
@@ -204,9 +222,8 @@
         spread(MOMENT)
 
     def spread_average():
-        wait(t_end.at[1], end2_sems.at[1])
-        for hf in both:
-            g[AVERAGE, hf, 0, 0] = ring2_close(1, hf).astype(BF16)
+        for hf in both:
+            g[AVERAGE, hf, 0, 0] = av[1, pl.ds(hf * half_rows, half_rows)].astype(BF16)
         spread(AVERAGE)
 
     def spread_step():
@@ -219,6 +236,10 @@
             g[STEP, hf, 0, 0] = (clipped + OUTER_MOMENTUM * moment).astype(BF16)
         spread(STEP)
 
+    def spread_far(s):
+        for hf in both:
+            gather1(s, hf, 3, 1)
+
     scales = {STEP: OUTER_RATE, MOMENT: OUTER_RATE * OUTER_MOMENTUM * OUTER_MOMENTUM}
 
     def clip_average():
@@ -255,20 +276,26 @@
             hand_over(s, hf, 1, 2, 1)
 
     def gather2_last(s):
-        wait(g.at[s, :, 3], gather_sems.at[s, 5])
-        for hf in both:
-            hand_over(s, hf, 3, 1, 2)
+        most = pl.ds(0, RING - 1)
+        wait(g.at[s, :, 3, most], gather_sems.at[s, 5])
+        for hf in both:
+            send(g.at[s, hf, 3, most], h.at[s, hf, 3, most], 7, hand_sems.at[s, 2], dev(0, 0, 1))
+
+    def gather2_end(s):
+        wait(g.at[s, :, 3, LAST], gather_sems.at[s, 6])
+        for hf in both:
+            send(g.at[s, hf, 3, LAST], h.at[s, hf, 3, LAST], 7, hand_sems.at[s, 3], dev(0, 0, 1))
 
     def hand_over(s, hf, slot, n, k):
         at = pl.ds(slot, n)
         send(g.at[s, hf, at], h.at[s, hf, at], 7, hand_sems.at[s, k], dev(0, 0, 1))
 
-    def refresh(s, hf, slot, blocks, c):
+    def refresh(s, hf, slot, blocks, c, first=0, last=RING):
         f = 0 if s == STEP else 1
         at = pl.ds(hf * half_rows, half_rows)
         scale = scales[s]
 
-        @pl.loop(0, RING)
+        @pl.loop(first, last)
         def _(j):
             col = pl.ds(column(hf, OFFSETS[slot], offset(j), c), width)
             gw[f, at, col] = gw[f, at, col] - scale * blocks[s, hf, slot, j].astype(F32)
@@ -279,11 +306,17 @@
                 refresh(s, hf, slot, g, core)
 
     def other(s, k):
-        slot, n = ((0, 1), (1, 2), (3, 1))[k]
-        wait(h.at[s, :, pl.ds(slot, n)], hand_sems.at[s, k])
-        for hf in both:
-            for i in range(n):
-                refresh(s, hf, slot + i, h, 1 - core)
+        if k < 2:
+            slot, n = ((0, 1), (1, 2))[k]
+            wait(h.at[s, :, pl.ds(slot, n)], hand_sems.at[s, k])
+            for hf in both:
+                for i in range(n):
+                    refresh(s, hf, slot + i, h, 1 - core)
+        else:
+            for k, first, last in ((2, 0, RING - 1), (3, RING - 1, RING)):
+                wait(h.at[s, :, 3, pl.ds(first, last - first)], hand_sems.at[s, k])
+                for hf in both:
+                    refresh(s, hf, 3, h, 1 - core, first, last)
 
     steps = []
 
@@ -295,9 +328,8 @@
             work(f, hf)
 
     def core_step(f, slot):
-        for hf in both:
-            if slot == 3:
-                load(f, hf)
+        load(f, slot)
+        for hf in both:
             to_core(f, slot, hf)
 
     def far_step(f):
@@ -330,6 +362,7 @@
     step(near_step, 0, 1)
     step(core_step, 0, 0)
     step(near_step, 0, 2)
+    step(known)
     step(core_step, 1, 3)
     step(core_step, 1, 1)
     step(core_step, 1, 2)
@@ -339,6 +372,7 @@
     step(near_step, 1, 1)
     step(near_step, 1, 2)
     step(middle_step, 1)
+    step(spread_far, MOMENT)
     step(open_step, 0)
     step(gather1_near, MOMENT)
     step(open_step, 1)
@@ -346,44 +380,48 @@
     step(norm_open, 0)
     step(gather1_far, MOMENT)
     step(gather2_first, MOMENT)
+    step(close_step, 1)
+    step(norm_open, 1)
+    step(spread_average)
     step(gather2_near, MOMENT)
-    step(spread_average)
     step(norm_middle, 0)
-    step(norm_open, 1)
     step(gather2_far, MOMENT)
     step(own, MOMENT, 0)
     step(gather1_near, AVERAGE)
+    step(gather1_far, AVERAGE)
+    step(spread_step)
+    step(gather2_first, AVERAGE)
     step(norm_middle, 1)
-    step(gather1_far, AVERAGE)
-    step(gather2_first, AVERAGE)
-    step(spread_step)
-    step(gather2_last, MOMENT)
-    step(other, MOMENT, 0)
     step(gather2_near, AVERAGE)
     step(gather2_far, AVERAGE)
     step(gather1_near, STEP)
     step(gather1_far, STEP)
-    step(own, MOMENT, 1)
     step(gather2_first, STEP)
-    step(clip_average)
-    step(own, MOMENT, 2, 3)
-    step(other, MOMENT, 1)
-    step(gather2_last, AVERAGE)
+    step(own, MOMENT, 1, 2)
     step(gather2_near, STEP)
     step(gather2_far, STEP)
+    step(gather2_last, MOMENT)
+    step(gather2_end, MOMENT)
+    step(other, MOMENT, 0)
+    step(other, MOMENT, 1)
+    step(own, MOMENT, 3)
+    step(clip_average)
+    step(gather2_last, AVERAGE)
+    step(gather2_end, AVERAGE)
     step(other, MOMENT, 2)
-    step(own, AVERAGE, 0, 1, 2)
+    step(own, AVERAGE, 0, 1, 2, 3)
     step(other, AVERAGE, 0)
+    step(other, AVERAGE, 1)
+    step(other, AVERAGE, 2)
+    step(gather2_last, STEP)
     step(own, STEP, 0)
-    step(gather2_last, STEP)
+    step(gather2_end, STEP)
     step(other, STEP, 0)
-    step(other, AVERAGE, 1)
-    step(own, AVERAGE, 3)
-    step(other, AVERAGE, 2)
     step(own, STEP, 1, 2)
     step(other, STEP, 1)
     step(own, STEP, 3)
     step(other, STEP, 2)
+
     for work, args in steps:
         work(*args)
 
@@ -427,16 +465,17 @@
             pltpu.VMEM((frags, RING * RING, 8, 128), F32),
             pltpu.VMEM((frags + 1, 2, RING, RING, half_rows, width), BF16),
             pltpu.VMEM((frags + 1, 2, RING, RING, half_rows, width), BF16),
-            dma((frags, 2, 2)),
+            dma((RING + 1, 2)),
             dma,
+            pltpu.SemaphoreType.REGULAR,
             dma((8,)),
             dma((frags, 2)),
             dma((frags, RING)),
             dma((frags,)),
             dma((frags,)),
             dma((frags,)),
-            dma((frags + 1, 6)),
-            dma((frags + 1, 3)),
+            dma((frags + 1, 7)),
+            dma((frags + 1, 4)),
         ],
         compiler_params=pltpu.CompilerParams(
             collective_id=0, has_side_effects=True, vmem_limit_bytes=50 * 2**20

time: 52.2 us -> 52.4 us (level)
  no operation moved by 1% of the time
where the time goes in v5:
time: 52.4 us; the launch traced here: 52.3 us
  Pallas kernels  47.6 us (91%)
  local copies, waits for them, and re-layouts  4.1 us (8%)
  between operations  0.64 us (1%)
    pallas_call x1, Pallas kernels, synchronize(): pl.pallas_call(functools.partial(kernel, zs, rows * zs * cols), out_shape...  47.6 us
    unnamed x2, local copies, waits for them, and re-layouts  4.1 us

profile of v5, /device:TPU:1, one launch (start us, length us, event | category | flops | bytes accessed | tf_op | source)
XLA Modules:
  0.0 52.3 jit_solution(9570939961981913014)
XLA Ops:
  0.6 47.6 %shard_map.50 = (f32[2,128,8192]{2,1,0:T(8,128)S(1)}, f32[2,128,256]{2,1,0:T(8,128)S(1)}) custom-call(bf16[1,2,128,8192]{3,2,1,0:T(8,128)(2,1)} %lw_hbm.1, f32[2,128,8192]{2,1,0:T(8,128)} %gw_hbm.1, f32[2,128,256]{2,1,0:T(8,128)} %mom_hbm.1), custom_call_target="tpu_custom_call" | custom-call | flops 20971520 | bytes 20971520 | tf_op jit(solution)/shard_map/pallas_call | solution.py:447
  48.2 3.4 %copy.7 = f32[2,128,8192]{2,1,0:T(8,128)} copy(f32[2,128,8192]{2,1,0:T(8,128)S(1)} %get-tuple-element.2) | data formatting | bytes 16777216
  51.6 0.7 %copy.8 = f32[2,128,256]{2,1,0:T(8,128)} copy(f32[2,128,256]{2,1,0:T(8,128)S(1)} %get-tuple-element.3) | data formatting | bytes 524288

commit v6 on v5

--- a/solution.py
+++ b/solution.py
@@ -17,8 +17,8 @@
 
 
 def kernel(zs, count, lw_hbm, gw_hbm, mom_hbm, gw, mout,
-           lw, mom, ds, dr, s_send, s_mid, s_end, tt, t_send, t_end, av, n1, n2, g, h,
-           in_sems, mom_sem, late_sem, send_sems, norm_sems, core_sems, mid_sems, end_sems, end2_sems, gather_sems, hand_sems):
+           lw, mom, ds, dr, s_send, s_mid, s_end, tt, t_send, t_end, av, n1, n2, g, h, p,
+           in_sems, mom_sem, late_sem, send_sems, norm_sems, core_sems, mid_sems, end_sems, end2_sems, gather_sems, hand_sems, share_sems):
     frags, rows, _ = gw.shape
     width = mom.shape[2]
     half_rows, quarter = rows // 2, rows // 4
@@ -215,11 +215,25 @@
         for hf in both:
             gather2(s, hf, FIRST, 2)
 
+    def share(i, *slots):
+        for hf in both:
+            for slot in slots:
+                back = (None, 2, 1, 3)[slot]
+                send(p.at[i, hf, 0], p.at[i, hf, back], 8, share_sems.at[i, slot // 3], along(1 - hf, OFFSETS[slot]))
+
+    def share_average():
+        for hf in both:
+            p[0, hf, 0] = av[0, pl.ds(hf * half_rows, half_rows)].astype(BF16)
+        share(0, 1, 2, 3)
+
     def spread_moment():
         mom_load.wait()
         for hf in both:
-            g[MOMENT, hf, 0, 0] = mom[1, pl.ds(hf * half_rows, half_rows)].astype(BF16)
+            at = pl.ds(hf * half_rows, half_rows)
+            g[MOMENT, hf, 0, 0] = mom[1, at].astype(BF16)
+            p[1, hf, 0] = mom[0, at].astype(BF16)
         spread(MOMENT)
+        share(1, 1, 2)
 
     def spread_average():
         for hf in both:
@@ -228,17 +242,24 @@
 
     def spread_step():
         factor = factor_of(0)
-        for hf in both:
-            at = pl.ds(hf * half_rows, half_rows)
-            clipped = av[0, at] * factor
-            moment = OUTER_MOMENTUM * mom[0, at] + clipped
-            mout[0, at] = moment
-            g[STEP, hf, 0, 0] = (clipped + OUTER_MOMENTUM * moment).astype(BF16)
-        spread(STEP)
+        for i in (1, 0):
+            wait(p.at[i, :, NEAR], share_sems.at[i, 0])
+            wait(p.at[i, :, LAST], share_sems.at[i, 1])
+        for at, slots, k in ((FIRST, (0,), 2), (NEAR, (1, 2), 3), (LAST, (3,), 4)):
+            for hf in both:
+                for slot in slots:
+                    clipped = p[0, hf, slot].astype(F32) * factor
+                    moment = OUTER_MOMENTUM * p[1, hf, slot].astype(F32) + clipped
+                    g[STEP, hf, 0, slot] = (clipped + OUTER_MOMENTUM * moment).astype(BF16)
+                gather2(STEP, hf, at, k)
+        for hf in both:
+            hand_over(STEP, hf, 0, 1, 0)
+        mout[0] = OUTER_MOMENTUM * mom[0] + av[0] * factor
 
     def spread_far(s):
         for hf in both:
             gather1(s, hf, 3, 1)
+        share(1, 3)
 
     scales = {STEP: OUTER_RATE, MOMENT: OUTER_RATE * OUTER_MOMENTUM * OUTER_MOMENTUM}
 
@@ -378,6 +399,7 @@
     step(open_step, 1)
     step(close_step, 0)
     step(norm_open, 0)
+    step(share_average)
     step(gather1_far, MOMENT)
     step(gather2_first, MOMENT)
     step(close_step, 1)
@@ -393,10 +415,8 @@
     step(gather2_first, AVERAGE)
     step(norm_middle, 1)
     step(gather2_near, AVERAGE)
+    step(gather2_first, STEP)
     step(gather2_far, AVERAGE)
-    step(gather1_near, STEP)
-    step(gather1_far, STEP)
-    step(gather2_first, STEP)
     step(own, MOMENT, 1, 2)
     step(gather2_near, STEP)
     step(gather2_far, STEP)
@@ -430,9 +450,10 @@
     wait(t_send, send_sems.at[2])
     wait(n1.at[:, pl.ds(0, len(near))], send_sems.at[3])
     wait(n2.at[:, pl.ds(0, len(far))], send_sems.at[4])
-    wait(g.at[:, :, 0, pl.ds(0, 3)], send_sems.at[5])
+    wait(g.at[pl.ds(1, frags), :, 0, pl.ds(0, 3)], send_sems.at[5])
     wait(g.at[:, :, pl.ds(0, 3)], send_sems.at[6])
     wait(h, send_sems.at[7])
+    wait(p.at[:, :, pl.ds(0, 3)], send_sems.at[8])
 
 
 def synchronize(local_weights, global_weights, momentum):
@@ -465,10 +486,11 @@
             pltpu.VMEM((frags, RING * RING, 8, 128), F32),
             pltpu.VMEM((frags + 1, 2, RING, RING, half_rows, width), BF16),
             pltpu.VMEM((frags + 1, 2, RING, RING, half_rows, width), BF16),
+            pltpu.VMEM((2, 2, RING, half_rows, width), BF16),
             dma((RING + 1, 2)),
             dma,
             pltpu.SemaphoreType.REGULAR,
-            dma((8,)),
+            dma((9,)),
             dma((frags, 2)),
             dma((frags, RING)),
             dma((frags,)),
@@ -476,6 +498,7 @@
             dma((frags,)),
             dma((frags + 1, 7)),
             dma((frags + 1, 4)),
+            dma((2, 2)),
         ],
         compiler_params=pltpu.CompilerParams(
             collective_id=0, has_side_effects=True, vmem_limit_bytes=50 * 2**20

time: 52.4 us -> 50.5 us (0.964)
  Pallas kernels: 47.6 us -> 45.6 us
    pallas_call x1, Pallas kernels: 47.6 us -> 45.6 us  [synchronize(): pl.pallas_call(functools.partial(kernel, zs, rows * zs * cols), out_shape...]
where the time goes in v6:
time: 50.5 us; the launch traced here: 50.4 us
  Pallas kernels  45.6 us (90%)
  local copies, waits for them, and re-layouts  4.1 us (8%)
  between operations  0.64 us (1%)
    pallas_call x1, Pallas kernels, synchronize(): pl.pallas_call(functools.partial(kernel, zs, rows * zs * cols), out_shape...  45.6 us
    unnamed x2, local copies, waits for them, and re-layouts  4.1 us

profile of v6, /device:TPU:1, one launch (start us, length us, event | category | flops | bytes accessed | tf_op | source)
XLA Modules:
  0.0 50.4 jit_solution(5451408383410323564)
XLA Ops:
  0.6 45.6 %shard_map.50 = (f32[2,128,8192]{2,1,0:T(8,128)S(1)}, f32[2,128,256]{2,1,0:T(8,128)S(1)}) custom-call(bf16[1,2,128,8192]{3,2,1,0:T(8,128)(2,1)} %lw_hbm.1, f32[2,128,8192]{2,1,0:T(8,128)} %gw_hbm.1, f32[2,128,256]{2,1,0:T(8,128)} %mom_hbm.1), custom_call_target="tpu_custom_call" | custom-call | flops 20971520 | bytes 20971520 | tf_op jit(solution)/shard_map/pallas_call | solution.py:468
  46.2 3.4 %copy.7 = f32[2,128,8192]{2,1,0:T(8,128)} copy(f32[2,128,8192]{2,1,0:T(8,128)S(1)} %get-tuple-element.2) | data formatting | bytes 16777216
  49.6 0.7 %copy.8 = f32[2,128,256]{2,1,0:T(8,128)} copy(f32[2,128,256]{2,1,0:T(8,128)S(1)} %get-tuple-element.3) | data formatting | bytes 524288

commit v7 on v5

--- a/solution.py
+++ b/solution.py
@@ -17,8 +17,8 @@
 
 
 def kernel(zs, count, lw_hbm, gw_hbm, mom_hbm, gw, mout,
-           lw, mom, ds, dr, s_send, s_mid, s_end, tt, t_send, t_end, av, n1, n2, g, h,
-           in_sems, mom_sem, late_sem, send_sems, norm_sems, core_sems, mid_sems, end_sems, end2_sems, gather_sems, hand_sems):
+           lw, mom, ds, dr, s_send, s_mid, s_end, tt, t_send, t_end, av, n1, n2, g, h, p,
+           in_sems, mom_sem, late_sem, send_sems, norm_sems, core_sems, mid_sems, end_sems, end2_sems, gather_sems, hand_sems, share_sems):
     frags, rows, _ = gw.shape
     width = mom.shape[2]
     half_rows, quarter = rows // 2, rows // 4
@@ -190,133 +190,105 @@
         norm_squared = jnp.sum(gathered(f, 0, n1, near), axis=(0, 1), keepdims=True)
         return jnp.minimum(1.0, CLIP_LEVEL * jnp.sqrt(F32(count)) / jnp.sqrt(norm_squared + 1e-06))
 
-    STEP, AVERAGE, MOMENT = 0, 1, 2
     FIRST, NEAR, LAST = pl.ds(0, 1), pl.ds(1, 2), pl.ds(3, 1)
 
-    def gather1(s, hf, slot, k):
-        back = (None, 2, 1, 3)[slot]
-        send(g.at[s, hf, 0, 0], g.at[s, hf, 0, back], 5, gather_sems.at[s, k], along(1 - hf, OFFSETS[slot]))
-
-    def gather2(s, hf, at, k):
+    def share(f, i, *slots):
+        for hf in both:
+            for slot in slots:
+                back = (None, 2, 1, 3)[slot]
+                send(p.at[f, i, hf, 0], p.at[f, i, hf, back], 5, share_sems.at[f, i, slot // 3],
+                     along(1 - hf, OFFSETS[slot]))
+
+    def share_average(f):
+        for hf in both:
+            p[f, 0, hf, 0] = av[f, pl.ds(hf * half_rows, half_rows)].astype(BF16)
+        share(f, 0, 1, 2, 3)
+
+    def share_moment(f):
+        for hf in both:
+            p[f, 1, hf, 0] = mom[f, pl.ds(hf * half_rows, half_rows)].astype(BF16)
+        share(f, 1, 1, 2)
+
+    def share_moment_far(f):
+        share(f, 1, 3)
+
+    def gather2(f, hf, at, k):
         for slot, back in ((1, 2), (2, 1)):
-            send(g.at[s, hf, 0, at], g.at[s, hf, back, at], 6, gather_sems.at[s, k], along(hf, OFFSETS[slot]))
-
-    def gather2_pass(s, hf, at, k):
-        k = 6 if k == 4 else 5
+            send(g.at[f, hf, 0, at], g.at[f, hf, back, at], 6, gather_sems.at[f, k], along(hf, OFFSETS[slot]))
+
+    def spread_step(f):
+        factor = factor_of(f)
+        for i in (1, 0):
+            wait(p.at[f, i, :, NEAR], share_sems.at[f, i, 0])
+            wait(p.at[f, i, :, LAST], share_sems.at[f, i, 1])
+        for k, at, slots in ((0, FIRST, (0,)), (1, NEAR, (1, 2)), (2, LAST, (3,))):
+            for hf in both:
+                for slot in slots:
+                    clipped = p[f, 0, hf, slot].astype(F32) * factor
+                    moment = OUTER_MOMENTUM * p[f, 1, hf, slot].astype(F32) + clipped
+                    g[f, hf, 0, slot] = (clipped + OUTER_MOMENTUM * moment).astype(BF16)
+                gather2(f, hf, at, k)
+        for hf in both:
+            hand_over(f, hf, 0, 1, 0)
+        mout[f] = OUTER_MOMENTUM * mom[f] + av[f] * factor
+
+    def gather2_pass(f, hf, at, k):
         for back, way, q in ((2, 1, 0), (1, -1, 1)):
             rows_at = pl.ds(q * quarter, quarter)
-            send(g.at[s, hf, back, at, rows_at], g.at[s, hf, 3, at, rows_at], 6,
-                 gather_sems.at[s, k], along(hf, way))
-
-    def spread(s):
-        for hf in both:
-            for slot in (1, 2, 3)[:2 if s == MOMENT else 3]:
-                gather1(s, hf, slot, slot // 3)
-        for hf in both:
-            gather2(s, hf, FIRST, 2)
-
-    def spread_moment():
-        mom_load.wait()
-        for hf in both:
-            g[MOMENT, hf, 0, 0] = mom[1, pl.ds(hf * half_rows, half_rows)].astype(BF16)
-        spread(MOMENT)
-
-    def spread_average():
-        for hf in both:
-            g[AVERAGE, hf, 0, 0] = av[1, pl.ds(hf * half_rows, half_rows)].astype(BF16)
-        spread(AVERAGE)
-
-    def spread_step():
-        factor = factor_of(0)
-        for hf in both:
-            at = pl.ds(hf * half_rows, half_rows)
-            clipped = av[0, at] * factor
-            moment = OUTER_MOMENTUM * mom[0, at] + clipped
-            mout[0, at] = moment
-            g[STEP, hf, 0, 0] = (clipped + OUTER_MOMENTUM * moment).astype(BF16)
-        spread(STEP)
-
-    def spread_far(s):
-        for hf in both:
-            gather1(s, hf, 3, 1)
-
-    scales = {STEP: OUTER_RATE, MOMENT: OUTER_RATE * OUTER_MOMENTUM * OUTER_MOMENTUM}
-
-    def clip_average():
-        factor = factor_of(1)
-        mout[1] = OUTER_MOMENTUM * mom[1] + av[1] * factor
-        scales[AVERAGE] = OUTER_RATE * (1.0 + OUTER_MOMENTUM) * factor
-
-    def gather1_near(s):
-        wait(g.at[s, :, 0, NEAR], gather_sems.at[s, 0])
-        for hf in both:
-            gather2(s, hf, NEAR, 3)
-
-    def gather1_far(s):
-        wait(g.at[s, :, 0, LAST], gather_sems.at[s, 1])
-        for hf in both:
-            gather2(s, hf, LAST, 4)
-        for hf in both:
-            hand_over(s, hf, 0, 1, 0)
-
-    def gather2_passes(s, at, k):
-        wait(g.at[s, :, pl.ds(1, 2), at], gather_sems.at[s, k])
-        for hf in both:
-            gather2_pass(s, hf, at, k)
-
-    def gather2_first(s):
-        gather2_passes(s, FIRST, 2)
-
-    def gather2_near(s):
-        gather2_passes(s, NEAR, 3)
-
-    def gather2_far(s):
-        gather2_passes(s, LAST, 4)
-        for hf in both:
-            hand_over(s, hf, 1, 2, 1)
-
-    def gather2_last(s):
+            send(g.at[f, hf, back, at, rows_at], g.at[f, hf, 3, at, rows_at], 6,
+                 gather_sems.at[f, 4 if k == 2 else 3], along(hf, way))
+
+    def gather2_passes(f, at, k):
+        wait(g.at[f, :, pl.ds(1, 2), at], gather_sems.at[f, k])
+        for hf in both:
+            gather2_pass(f, hf, at, k)
+
+    def gather2_first(f):
+        gather2_passes(f, FIRST, 0)
+
+    def gather2_near(f):
+        gather2_passes(f, NEAR, 1)
+
+    def gather2_far(f):
+        gather2_passes(f, LAST, 2)
+        for hf in both:
+            hand_over(f, hf, 1, 2, 1)
+
+    def gather2_last(f):
         most = pl.ds(0, RING - 1)
-        wait(g.at[s, :, 3, most], gather_sems.at[s, 5])
-        for hf in both:
-            send(g.at[s, hf, 3, most], h.at[s, hf, 3, most], 7, hand_sems.at[s, 2], dev(0, 0, 1))
-
-    def gather2_end(s):
-        wait(g.at[s, :, 3, LAST], gather_sems.at[s, 6])
-        for hf in both:
-            send(g.at[s, hf, 3, LAST], h.at[s, hf, 3, LAST], 7, hand_sems.at[s, 3], dev(0, 0, 1))
-
-    def hand_over(s, hf, slot, n, k):
+        wait(g.at[f, :, 3, most], gather_sems.at[f, 3])
+        for hf in both:
+            send(g.at[f, hf, 3, most], h.at[f, hf, 3, most], 7, hand_sems.at[f, 2], dev(0, 0, 1))
+
+    def gather2_end(f):
+        wait(g.at[f, :, 3, LAST], gather_sems.at[f, 4])
+        for hf in both:
+            send(g.at[f, hf, 3, LAST], h.at[f, hf, 3, LAST], 7, hand_sems.at[f, 3], dev(0, 0, 1))
+
+    def hand_over(f, hf, slot, n, k):
         at = pl.ds(slot, n)
-        send(g.at[s, hf, at], h.at[s, hf, at], 7, hand_sems.at[s, k], dev(0, 0, 1))
-
-    def refresh(s, hf, slot, blocks, c, first=0, last=RING):
-        f = 0 if s == STEP else 1
+        send(g.at[f, hf, at], h.at[f, hf, at], 7, hand_sems.at[f, k], dev(0, 0, 1))
+
+    def refresh(f, hf, slot, blocks, c, first=0, last=RING):
         at = pl.ds(hf * half_rows, half_rows)
-        scale = scales[s]
 
         @pl.loop(first, last)
         def _(j):
             col = pl.ds(column(hf, OFFSETS[slot], offset(j), c), width)
-            gw[f, at, col] = gw[f, at, col] - scale * blocks[s, hf, slot, j].astype(F32)
-
-    def own(s, *slots):
+            gw[f, at, col] = gw[f, at, col] - OUTER_RATE * blocks[f, hf, slot, j].astype(F32)
+
+    def own(f, *slots):
         for hf in both:
             for slot in slots:
-                refresh(s, hf, slot, g, core)
-
-    def other(s, k):
-        if k < 2:
-            slot, n = ((0, 1), (1, 2))[k]
-            wait(h.at[s, :, pl.ds(slot, n)], hand_sems.at[s, k])
-            for hf in both:
-                for i in range(n):
-                    refresh(s, hf, slot + i, h, 1 - core)
-        else:
-            for k, first, last in ((2, 0, RING - 1), (3, RING - 1, RING)):
-                wait(h.at[s, :, 3, pl.ds(first, last - first)], hand_sems.at[s, k])
-                for hf in both:
-                    refresh(s, hf, 3, h, 1 - core, first, last)
+                refresh(f, hf, slot, g, core)
+
+    def other(f, k):
+        slot, n = ((0, 1), (1, 2), (3, 1), (3, 1))[k]
+        first, last = ((0, RING), (0, RING), (0, RING - 1), (RING - 1, RING))[k]
+        wait(h.at[f, :, pl.ds(slot, n), pl.ds(first, last - first)], hand_sems.at[f, k])
+        for hf in both:
+            for i in range(n):
+                refresh(f, hf, slot + i, h, 1 - core, first, last)
 
     steps = []
 
@@ -354,7 +326,9 @@
         wait(t_end.at[f], end2_sems.at[f])
         halves(ring2_close, f)
 
-    step(spread_moment)
+    step(mom_load.wait)
+    step(share_moment, 0)
+    step(share_moment, 1)
     step(core_step, 0, 3)
     step(core_step, 0, 1)
     step(far_step, 0)
@@ -372,56 +346,45 @@
     step(near_step, 1, 1)
     step(near_step, 1, 2)
     step(middle_step, 1)
-    step(spread_far, MOMENT)
     step(open_step, 0)
-    step(gather1_near, MOMENT)
     step(open_step, 1)
     step(close_step, 0)
     step(norm_open, 0)
-    step(gather1_far, MOMENT)
-    step(gather2_first, MOMENT)
+    step(share_average, 0)
+    step(share_moment_far, 0)
     step(close_step, 1)
     step(norm_open, 1)
-    step(spread_average)
-    step(gather2_near, MOMENT)
+    step(share_average, 1)
+    step(share_moment_far, 1)
     step(norm_middle, 0)
-    step(gather2_far, MOMENT)
-    step(own, MOMENT, 0)
-    step(gather1_near, AVERAGE)
-    step(gather1_far, AVERAGE)
-    step(spread_step)
-    step(gather2_first, AVERAGE)
     step(norm_middle, 1)
-    step(gather2_near, AVERAGE)
-    step(gather2_far, AVERAGE)
-    step(gather1_near, STEP)
-    step(gather1_far, STEP)
-    step(gather2_first, STEP)
-    step(own, MOMENT, 1, 2)
-    step(gather2_near, STEP)
-    step(gather2_far, STEP)
-    step(gather2_last, MOMENT)
-    step(gather2_end, MOMENT)
-    step(other, MOMENT, 0)
-    step(other, MOMENT, 1)
-    step(own, MOMENT, 3)
-    step(clip_average)
-    step(gather2_last, AVERAGE)
-    step(gather2_end, AVERAGE)
-    step(other, MOMENT, 2)
-    step(own, AVERAGE, 0, 1, 2, 3)
-    step(other, AVERAGE, 0)
-    step(other, AVERAGE, 1)
-    step(other, AVERAGE, 2)
-    step(gather2_last, STEP)
-    step(own, STEP, 0)
-    step(gather2_end, STEP)
-    step(other, STEP, 0)
-    step(own, STEP, 1, 2)
-    step(other, STEP, 1)
-    step(own, STEP, 3)
-    step(other, STEP, 2)
-
+    step(spread_step, 0)
+    step(gather2_first, 0)
+    step(spread_step, 1)
+    step(gather2_near, 0)
+    step(gather2_far, 0)
+    step(own, 0, 0)
+    step(gather2_first, 1)
+    step(gather2_last, 0)
+    step(gather2_end, 0)
+    step(gather2_near, 1)
+    step(gather2_far, 1)
+    step(other, 0, 0)
+    step(own, 0, 1, 2)
+    step(own, 1, 0)
+    step(other, 0, 1)
+    step(other, 1, 0)
+    step(own, 0, 3)
+    step(other, 0, 2)
+    step(other, 0, 3)
+    step(gather2_last, 1)
+    step(own, 1, 1)
+    step(gather2_end, 1)
+    step(own, 1, 2)
+    step(other, 1, 1)
+    step(own, 1, 3)
+    step(other, 1, 2)
+    step(other, 1, 3)
     for work, args in steps:
         work(*args)
 
@@ -430,7 +393,7 @@
     wait(t_send, send_sems.at[2])
     wait(n1.at[:, pl.ds(0, len(near))], send_sems.at[3])
     wait(n2.at[:, pl.ds(0, len(far))], send_sems.at[4])
-    wait(g.at[:, :, 0, pl.ds(0, 3)], send_sems.at[5])
+    wait(p.at[:, :, :, pl.ds(0, 3)], send_sems.at[5])
     wait(g.at[:, :, pl.ds(0, 3)], send_sems.at[6])
     wait(h, send_sems.at[7])
 
@@ -463,8 +426,9 @@
             pltpu.VMEM((frags, rows, width), F32),
             pltpu.VMEM((frags, 2 * zs, 8, 128), F32),
             pltpu.VMEM((frags, RING * RING, 8, 128), F32),
-            pltpu.VMEM((frags + 1, 2, RING, RING, half_rows, width), BF16),
-            pltpu.VMEM((frags + 1, 2, RING, RING, half_rows, width), BF16),
+            pltpu.VMEM((frags, 2, RING, RING, half_rows, width), BF16),
+            pltpu.VMEM((frags, 2, RING, RING, half_rows, width), BF16),
+            pltpu.VMEM((frags, 2, 2, RING, half_rows, width), BF16),
             dma((RING + 1, 2)),
             dma,
             pltpu.SemaphoreType.REGULAR,
@@ -474,8 +438,9 @@
             dma((frags,)),
             dma((frags,)),
             dma((frags,)),
-            dma((frags + 1, 7)),
-            dma((frags + 1, 4)),
+            dma((frags, 5)),
+            dma((frags, 4)),
+            dma((frags, 2, 2)),
         ],
         compiler_params=pltpu.CompilerParams(
             collective_id=0, has_side_effects=True, vmem_limit_bytes=50 * 2**20

time: 52.4 us -> 52.5 us (level)
  no operation moved by 1% of the time
where the time goes in v7:
time: 52.5 us; the launch traced here: 52.4 us
  Pallas kernels  47.7 us (91%)
  local copies, waits for them, and re-layouts  4.1 us (8%)
  between operations  0.64 us (1%)
    pallas_call x1, Pallas kernels, synchronize(): pl.pallas_call(functools.partial(kernel, zs, rows * zs * cols), out_shape...  47.7 us
    unnamed x2, local copies, waits for them, and re-layouts  4.1 us

profile of v7, /device:TPU:1, one launch (start us, length us, event | category | flops | bytes accessed | tf_op | source)
XLA Modules:
  0.0 52.4 jit_solution(13608577808367351798)
XLA Ops:
  0.6 47.7 %shard_map.50 = (f32[2,128,8192]{2,1,0:T(8,128)S(1)}, f32[2,128,256]{2,1,0:T(8,128)S(1)}) custom-call(bf16[1,2,128,8192]{3,2,1,0:T(8,128)(2,1)} %lw_hbm.1, f32[2,128,8192]{2,1,0:T(8,128)} %gw_hbm.1, f32[2,128,256]{2,1,0:T(8,128)} %mom_hbm.1), custom_call_target="tpu_custom_call" | custom-call | flops 20971520 | bytes 20971520 | tf_op jit(solution)/shard_map/pallas_call | solution.py:410
  48.3 3.4 %copy.7 = f32[2,128,8192]{2,1,0:T(8,128)} copy(f32[2,128,8192]{2,1,0:T(8,128)S(1)} %get-tuple-element.2) | data formatting | bytes 16777216
  51.7 0.7 %copy.8 = f32[2,128,256]{2,1,0:T(8,128)} copy(f32[2,128,256]{2,1,0:T(8,128)S(1)} %get-tuple-element.3) | data formatting | bytes 524288

commit v8 on v6

--- a/solution.py
+++ b/solution.py
@@ -12,6 +12,7 @@
 CLIP_LEVEL = 1.0
 MESH = pl.DeviceIdType.MESH
 RING = 4
+PARTS = 2
 OFFSETS = (0, 1, -1, 2)
 F32, BF16 = jnp.float32, jnp.bfloat16
 
@@ -456,6 +457,20 @@
     wait(p.at[:, :, pl.ds(0, 3)], send_sems.at[8])
 
 
+def store(refreshed, moment, refreshed_out, moment_out, sems):
+    frags, rows, _ = refreshed.shape
+    n = rows // PARTS
+    copies = [pltpu.make_async_copy(moment, moment_out, sems.at[frags * PARTS])]
+    for f in range(frags):
+        for i in range(PARTS):
+            at = pl.ds(i * n, n)
+            copies.append(pltpu.make_async_copy(refreshed.at[f, at], refreshed_out.at[f, at], sems.at[f * PARTS + i]))
+    for copy in copies:
+        copy.start()
+    for copy in copies:
+        copy.wait()
+
+
 def synchronize(local_weights, global_weights, momentum):
     frags, rows, cols = global_weights.shape
     width = momentum.shape[2]
@@ -465,7 +480,7 @@
     anywhere = pl.BlockSpec(memory_space=pl.ANY)
     in_vmem = pl.BlockSpec(memory_space=pltpu.VMEM)
     dma = pltpu.SemaphoreType.DMA
-    return pl.pallas_call(
+    refreshed, moment = pl.pallas_call(
         functools.partial(kernel, zs, rows * zs * cols),
         out_shape=(pltpu.VMEM(global_weights.shape, F32), pltpu.VMEM(momentum.shape, F32)),
         in_specs=[anywhere] * 3,
@@ -505,6 +520,17 @@
         ),
         cost_estimate=pl.CostEstimate(flops=20 * rows * cols, bytes_accessed=20 * frags * rows * cols // 2, transcendentals=0),
     )(local_weights, global_weights, momentum)
+    return pl.pallas_call(
+        store,
+        out_shape=(
+            jax.ShapeDtypeStruct(global_weights.shape, F32),
+            jax.ShapeDtypeStruct(momentum.shape, F32),
+        ),
+        in_specs=[in_vmem, in_vmem],
+        out_specs=(anywhere, anywhere),
+        scratch_shapes=[dma((frags * PARTS + 1,))],
+        compiler_params=pltpu.CompilerParams(vmem_limit_bytes=2 * 2**20),
+    )(refreshed, moment)
 
 
 def solution(mesh):

time: 50.5 us -> 49.8 us (0.986)
  local copies, waits for them, and re-layouts: 4.1 us -> 0 us
  Pallas kernels: 45.6 us -> 49.1 us
    unnamed x2 -> x0, local copies, waits for them, and re-layouts: 4.1 us -> none
    pallas_call x0 -> x1, Pallas kernels: none -> 3.46 us  [synchronize(): pl.pallas_call(store, out_shape=(jax.ShapeDtypeStruct(global_weights.shap...]
where the time goes in v8:
time: 49.8 us; the launch traced here: 49.7 us
  Pallas kernels  49.1 us (99%)
  between operations  0.64 us (1%)
    pallas_call x1, Pallas kernels, synchronize(): pl.pallas_call(functools.partial(kernel, zs, rows * zs * cols), out_shape...  45.6 us
    pallas_call x1, Pallas kernels, synchronize(): pl.pallas_call(store, out_shape=(jax.ShapeDtypeStruct(global_weights.shap...  3.46 us

profile of v8, /device:TPU:1, one launch (start us, length us, event | category | flops | bytes accessed | tf_op | source)
XLA Modules:
  0.0 49.7 jit_solution(886726088808622356)
XLA Ops:
  0.6 45.6 %shard_map.50 = (f32[2,128,8192]{2,1,0:T(8,128)S(1)}, f32[2,128,256]{2,1,0:T(8,128)S(1)}) custom-call(bf16[1,2,128,8192]{3,2,1,0:T(8,128)(2,1)} %lw_hbm.1, f32[2,128,8192]{2,1,0:T(8,128)} %gw_hbm.1, f32[2,128,256]{2,1,0:T(8,128)} %mom_hbm.1), custom_call_target="tpu_custom_call" | custom-call | flops 20971520 | bytes 20971520 | tf_op jit(solution)/shard_map/pallas_call | solution.py:483
  46.2 3.5 %shard_map.51 = (f32[2,128,8192]{2,1,0:T(8,128)}, f32[2,128,256]{2,1,0:T(8,128)}) custom-call(f32[2,128,8192]{2,1,0:T(8,128)S(1)} %get-tuple-element.4.refreshed, f32[2,128,256]{2,1,0:T(8,128)S(1)} %get-tuple-element.5.moment), custom_call_target="tpu_custom_call" | custom-call | tf_op jit(solution)/shard_map/pallas_call | solution.py:523

commit v9 on v8

--- a/solution.py
+++ b/solution.py
@@ -391,55 +391,56 @@
     step(far_step, 1)
     step(core_step, 1, 0)
     step(middle_step, 0)
+    step(spread_far, MOMENT)
     step(near_step, 1, 1)
     step(near_step, 1, 2)
     step(middle_step, 1)
-    step(spread_far, MOMENT)
     step(open_step, 0)
     step(gather1_near, MOMENT)
+    step(gather1_far, MOMENT)
     step(open_step, 1)
     step(close_step, 0)
     step(norm_open, 0)
     step(share_average)
-    step(gather1_far, MOMENT)
     step(gather2_first, MOMENT)
     step(close_step, 1)
+    step(spread_average)
     step(norm_open, 1)
-    step(spread_average)
     step(gather2_near, MOMENT)
     step(norm_middle, 0)
     step(gather2_far, MOMENT)
     step(own, MOMENT, 0)
     step(gather1_near, AVERAGE)
     step(gather1_far, AVERAGE)
+    step(own, MOMENT, 1)
+    step(gather2_first, AVERAGE)
     step(spread_step)
-    step(gather2_first, AVERAGE)
-    step(norm_middle, 1)
-    step(gather2_near, AVERAGE)
-    step(gather2_first, STEP)
-    step(gather2_far, AVERAGE)
-    step(own, MOMENT, 1, 2)
-    step(gather2_near, STEP)
-    step(gather2_far, STEP)
+    step(own, MOMENT, 2)
     step(gather2_last, MOMENT)
     step(gather2_end, MOMENT)
     step(other, MOMENT, 0)
+    step(gather2_near, AVERAGE)
+    step(norm_middle, 1)
+    step(gather2_first, STEP)
+    step(gather2_far, AVERAGE)
     step(other, MOMENT, 1)
     step(own, MOMENT, 3)
+    step(gather2_near, STEP)
+    step(gather2_far, STEP)
+    step(other, MOMENT, 2)
     step(clip_average)
+    step(own, AVERAGE, 0, 1, 2)
+    step(other, AVERAGE, 0)
     step(gather2_last, AVERAGE)
     step(gather2_end, AVERAGE)
-    step(other, MOMENT, 2)
-    step(own, AVERAGE, 0, 1, 2, 3)
-    step(other, AVERAGE, 0)
+    step(own, STEP, 0, 1, 2)
+    step(other, STEP, 0)
     step(other, AVERAGE, 1)
+    step(gather2_last, STEP)
+    step(own, AVERAGE, 3)
+    step(gather2_end, STEP)
+    step(other, STEP, 1)
     step(other, AVERAGE, 2)
-    step(gather2_last, STEP)
-    step(own, STEP, 0)
-    step(gather2_end, STEP)
-    step(other, STEP, 0)
-    step(own, STEP, 1, 2)
-    step(other, STEP, 1)
     step(own, STEP, 3)
     step(other, STEP, 2)
 

time: 49.8 us -> 49.4 us (level)
  no operation moved by 1% of the time
where the time goes in v9:
time: 49.4 us; the launch traced here: 49.3 us
  Pallas kernels  48.7 us (99%)
  between operations  0.64 us (1%)
    pallas_call x1, Pallas kernels, synchronize(): pl.pallas_call(functools.partial(kernel, zs, rows * zs * cols), out_shape...  45.2 us
    pallas_call x1, Pallas kernels, synchronize(): pl.pallas_call(store, out_shape=(jax.ShapeDtypeStruct(global_weights.shap...  3.46 us

profile of v9, /device:TPU:1, one launch (start us, length us, event | category | flops | bytes accessed | tf_op | source)
XLA Modules:
  0.0 49.3 jit_solution(14631542368972398148)
XLA Ops:
  0.6 45.2 %shard_map.50 = (f32[2,128,8192]{2,1,0:T(8,128)S(1)}, f32[2,128,256]{2,1,0:T(8,128)S(1)}) custom-call(bf16[1,2,128,8192]{3,2,1,0:T(8,128)(2,1)} %lw_hbm.1, f32[2,128,8192]{2,1,0:T(8,128)} %gw_hbm.1, f32[2,128,256]{2,1,0:T(8,128)} %mom_hbm.1), custom_call_target="tpu_custom_call" | custom-call | flops 20971520 | bytes 20971520 | tf_op jit(solution)/shard_map/pallas_call | solution.py:484
  45.9 3.5 %shard_map.51 = (f32[2,128,8192]{2,1,0:T(8,128)}, f32[2,128,256]{2,1,0:T(8,128)}) custom-call(f32[2,128,8192]{2,1,0:T(8,128)S(1)} %get-tuple-element.4.refreshed, f32[2,128,256]{2,1,0:T(8,128)S(1)} %get-tuple-element.5.moment), custom_call_target="tpu_custom_call" | custom-call | tf_op jit(solution)/shard_map/pallas_call | solution.py:524

commit v10 on v9

--- a/solution.py
+++ b/solution.py
@@ -80,15 +80,14 @@
             for copy in later:
                 copy.wait()
 
-    start_load(3)
-    mom_load.start()
-
     near = [(0, 0, oc, oz) for oz in range(zs) for oc in range(2) if (oc, oz) != (0, 0)]
     far = [(ox, oy, 0, 0) for ox in range(RING) for oy in range(RING) if (ox, oy) != (0, 0)]
     greeted = [(0, 0, 1, 0)] + [p for o in (1, -1) for p in ((o, 0, 0, 0), (0, o, 0, 0), (0, 0, 0, o))]
     barrier = pltpu.get_barrier_semaphore()
     for partner in greeted:
         pl.semaphore_signal(barrier, inc=1, device_id=dev(*partner), device_id_type=MESH)
+    start_load(3)
+    mom_load.start()
     for slot in (1, 2, 0):
         start_load(slot)
     pl.semaphore_wait(barrier, len(greeted))

time: 49.4 us -> 49.8 us (level)
  no operation moved by 1% of the time
where the time goes in v10:
time: 49.8 us; the launch traced here: 49.7 us
  Pallas kernels  49 us (98%)
  between operations  0.64 us (1%)
    pallas_call x1, Pallas kernels, synchronize(): pl.pallas_call(functools.partial(kernel, zs, rows * zs * cols), out_shape...  45.6 us
    pallas_call x1, Pallas kernels, synchronize(): pl.pallas_call(store, out_shape=(jax.ShapeDtypeStruct(global_weights.shap...  3.46 us

profile of v10, /device:TPU:1, one launch (start us, length us, event | category | flops | bytes accessed | tf_op | source)
XLA Modules:
  0.0 49.7 jit_solution(1123686574873488668)
XLA Ops:
  0.6 45.6 %shard_map.50 = (f32[2,128,8192]{2,1,0:T(8,128)S(1)}, f32[2,128,256]{2,1,0:T(8,128)S(1)}) custom-call(bf16[1,2,128,8192]{3,2,1,0:T(8,128)(2,1)} %lw_hbm.1, f32[2,128,8192]{2,1,0:T(8,128)} %gw_hbm.1, f32[2,128,256]{2,1,0:T(8,128)} %mom_hbm.1), custom_call_target="tpu_custom_call" | custom-call | flops 20971520 | bytes 20971520 | tf_op jit(solution)/shard_map/pallas_call | solution.py:483
  46.2 3.5 %shard_map.51 = (f32[2,128,8192]{2,1,0:T(8,128)}, f32[2,128,256]{2,1,0:T(8,128)}) custom-call(f32[2,128,8192]{2,1,0:T(8,128)S(1)} %get-tuple-element.4.refreshed, f32[2,128,256]{2,1,0:T(8,128)S(1)} %get-tuple-element.5.moment), custom_call_target="tpu_custom_call" | custom-call | tf_op jit(solution)/shard_map/pallas_call | solution.py:523
